TPU v7x, 512 devices: a whole 4x8x8 slice. The times are simulated.
512 devices in a mesh: grp: 32 (over y, x_hi, core), span: 16 (over z, x_lo).
Axes of the slice: x: 4 (x_hi: 2, x_lo: 2; x = x_hi * 2 + x_lo), y: 8, z: 8, core: 2. Of those that a mesh axis runs over, the one named last changes fastest.
Arguments:
- strain: bfloat16 [8192, 49152], P('grp', 'span'), may hold values from -60 to 60
- channel_map: int32 [32, 256], P('grp'), may hold values from 0 to 255, each once within a row
- bin_index: int32 [64], replicated, may hold values from 1 to 511
Outputs:
- cross_spectra: bfloat16 [3, 64, 8192, 512], P(None, 'span', 'grp')
All inputs are finite; a program needn't handle non-finite values.
Results may differ from a plain program's by a relative error of at most 0.0064.
Values may be sent and summed in bfloat16 or wider, within the bound.
A program may use at most 64 MiB of HBM per device.

v0:
```python
import math

import jax
import jax.numpy as jnp
from jax import lax
from jax.sharding import PartitionSpec as P

W = 1024
ROUNDS = 3


epsilon = 1e-06


def from_behind(x, axis, by):
    count = lax.axis_size(axis)
    pairs = [(i, i + by) for i in range(count) if 0 <= i + by < count]
    return lax.ppermute(x, axis, pairs)


def from_behind_2(block, axis, distance):
    devices = range(lax.axis_size(axis))
    route = [((i - distance) % len(devices), i) for i in devices]
    return lax.ppermute(block, axis, route)


def dft_table(bin_index, length):
    sample_ids = jnp.arange(length, dtype=jnp.int32)
    phase_int = sample_ids[:, None] * bin_index[None, :] % length
    angles = phase_int.astype(jnp.float32) * (2.0 * math.pi / length)
    hann_taper = 0.5 - 0.5 * jnp.cos(sample_ids.astype(jnp.float32) * (2.0 * math.pi / length))
    cos_sin = jnp.stack([jnp.cos(angles), -jnp.sin(angles)], axis=-1)
    return (
        (hann_taper[:, None, None] * cos_sin)
        .reshape(length, 2 * bin_index.shape[0])
        .astype(jnp.bfloat16)
    )


def cross_block(local_block, partner, stack_scale):
    half_len = partner.shape[1] // 2
    turned = jnp.concatenate([-partner[:, half_len:], partner[:, :half_len]], axis=1)
    right_operand = jnp.concatenate([partner, turned], axis=2)
    spectral_product = jnp.einsum(
        "swu,swe->sue", local_block, right_operand, preferred_element_type=jnp.float32
    )
    return (spectral_product * stack_scale).astype(jnp.bfloat16)


def local(strain, channel_map, bin_index):
    hop_len = W // 4
    group_size = strain.shape[0]
    win_local = strain.shape[1] // hop_len
    slab_count = lax.axis_size("span")
    windows = win_local * slab_count
    bin_count = bin_index.shape[0]
    per_slab = bin_count // slab_count
    ordered = jnp.take(strain, channel_map[0], axis=0)
    next_tail = from_behind(ordered[:, : 3 * hop_len], "span", -1)
    extended = jnp.concatenate([ordered, next_tail], axis=1).reshape(
        group_size, win_local + 3, hop_len
    )
    fourier_basis_matrix = dft_table(bin_index, W).reshape(4, hop_len, 2 * bin_count)
    window_spectra = jnp.zeros((2 * bin_count, win_local, group_size), jnp.float32)
    for quarter in range(4):
        window_spectra = window_spectra + jnp.einsum(
            "chs,sk->khc",
            extended[:, quarter : quarter + win_local],
            fourier_basis_matrix[quarter],
            preferred_element_type=jnp.float32,
        )
    rounded = window_spectra.astype(jnp.bfloat16)
    slab_data = lax.all_to_all(rounded, "span", split_axis=0, concat_axis=1, tiled=True)
    values = slab_data.astype(jnp.float32).reshape(per_slab, 2, windows, group_size)
    power_mean = jnp.mean(values * values, axis=(1, 2))
    whitened = (values * lax.rsqrt(power_mean + epsilon)[:, None, None, :]).astype(jnp.bfloat16)
    whitened = whitened.reshape(per_slab, 2 * windows, group_size)
    stack_scale = 1.0 / math.sqrt(windows)
    results = []
    for offset in range(1, ROUNDS + 1):
        partner = from_behind_2(whitened, "grp", -offset)
        results.append(cross_block(whitened, partner, stack_scale))
    return jnp.stack(results, axis=0)


def solution(mesh):
    return jax.shard_map(
        local,
        mesh=mesh,
        in_specs=(P("grp", "span"), P("grp", None), P()),
        out_specs=P(None, "span", "grp", None),
        check_vma=False,
    )
```

profile of v0, /device:TPU:29, one launch (start us, length us, event | category | flops | bytes accessed | tf_op | source)
XLA Modules:
  0.0 123.4 jit_solution(9124368142164142131)
XLA Ops:
  0.0 0.8 compare_select_fusion
  0.8 0.7 compare_and_fusion
  1.5 2.7 %gather_fusion = bf16[256,3072]{1,0:T(8,128)(2,1)} fusion(bf16[256,3072]{1,0:T(8,128)(2,1)S(1)} %copy-done, s32[1024]{0:T(1024)S(1)} %pad_clamp_fusion), kind=kCustom, calls=%fused_computation | custom fusion | bytes 3146752 | tf_op jit(solution)/shard_map/jit(_take)/gather | solution.py:58
  4.2 1.6 %broadcast_select_fusion = bf16[256,3072]{1,0:T(8,128)(2,1)S(1)} fusion(bf16[256,3072]{1,0:T(8,128)(2,1)} %gather_fusion, pred[256]{0:T(512)(128)(4,1)S(1)} %compare_and_fusion), kind=kLoop, calls=%fused_computation.33 | loop fusion | flops 786432 | bytes 3145984 | tf_op jit(solution)/shard_map/jit(_take)/select_n | solution.py:58
  5.9 1.3 %collective-permute-start = (bf16[256,768]{1,0:T(8,128)(2,1)S(1)}, bf16[256,768]{1,0:T(8,128)(2,1)}, u32[]{:S(2)}, u32[]{:S(2)}) collective-permute-start(bf16[256,768]{1,0:T(8,128)(2,1)S(1)} %slice.67), channel_id=1, source_target_pairs={{1,0},{2,1},{3,2},{4,3},{5,4},{6,5},{7,6},{8,7},{9,8},{10,9},{11,1... | collective-permute-start | bytes 1179656 | tf_op jit(solution)/shard_map/ppermute | solution.py:18
  7.2 1.1 fusion.43
  8.4 1.2 copy.49
  9.6 2.2 %stack.20 = f32[1024,128]{0,1:T(8,128)} reshape(f32[1024,64,2]{0,2,1:T(2,128)} %copy.49) | data formatting | bytes 1048576 | tf_op jit(solution)/shard_map/stack | solution.py:32
  11.8 1.8 %multiply_convert_fusion.4 = bf16[1024,128]{0,1:T(8,128)(2,1)} fusion(f32[1024,128]{0,1:T(8,128)} %stack.20, f32[1024]{0:T(1024)S(1)} %multiply_subtract_fusion), kind=kLoop, calls=%fused_computation.39 | loop fusion | flops 262144 | bytes 790528 | tf_op jit(solution)/shard_map/convert_element_type | solution.py:36
  13.6 4.3 %collective-permute-done = bf16[256,768]{1,0:T(8,128)(2,1)} collective-permute-done((bf16[256,768]{1,0:T(8,128)(2,1)S(1)}, bf16[256,768]{1,0:T(8,128)(2,1)}, u32[]{:S(2)}, u32[]{:S(2)}) %collective-permute-start) | collective-permute-done | bytes 393248 | tf_op jit(solution)/shard_map/ppermute | solution.py:18
  17.9 2.4 %pad_maximum_fusion.1 = bf16[256,3840]{1,0:T(8,128)(2,1)} fusion(bf16[256,768]{1,0:T(8,128)(2,1)} %collective-permute-done, bf16[256,3072]{1,0:T(8,128)(2,1)S(1)} %broadcast_select_fusion), kind=kLoop, calls=%fused_computation.7 | loop fusion | flops 3932160 | bytes 3932160 | tf_op jit(solution)/shard_map/concatenate | solution.py:60
  20.3 2.7 %copy.50 = bf16[256,3840]{0,1:T(8,128)(2,1)S(1)} copy(bf16[256,3840]{1,0:T(8,128)(2,1)} %pad_maximum_fusion.1) | data formatting | bytes 3932160 | tf_op jit(solution)/shard_map/concatenate | solution.py:60
  23.0 1.3 %fusion.2 = f32[128,256,12]{1,0,2:T(8,128)S(1)} fusion(bf16[256,15,256]{0,2,1:T(8,128)(2,1)S(1)} %bitcast.36, bf16[1024,128]{0,1:T(8,128)(2,1)} %multiply_convert_fusion.4), kind=kOutput, calls=%fused_computation.10 | convolution fusion | flops 201326592 | bytes 3211264 | tf_op jit(solution)/shard_map/chs,sk->khc/dot_general | solution.py:66
  24.3 0.4 fusion.4
  24.6 0.4 fusion.6
  25.0 0.6 fusion.34
  25.6 0.5 copy.55
  26.1 37.6 %all_to_all.4 = bf16[128,12,256]{2,1,0:T(8,128)(2,1)S(1)} all-to-all(bf16[128,12,256]{2,1,0:T(8,128)(2,1)S(1)} %copy.55), channel_id=1, replica_groups=mesh['grp'=32,'span'=16] {'span'}, dimensions={0} | all-to-all | bytes 1572864 | tf_op jit(solution)/shard_map/all_to_all | solution.py:73
  63.7 0.5 multiply_reduce_fusion
  64.3 1.6 %copy_bitcast_fusion = f32[8,16,12,256]{3,2,1,0:T(8,128)} fusion(bf16[16,8,12,256]{3,2,1,0:T(8,128)(2,1)S(1)} %bitcast.40), kind=kLoop, calls=%fused_computation.2 | loop fusion | flops 393216 | bytes 2359296 | tf_op jit(solution)/shard_map/convert_element_type | solution.py:74
  65.9 1.6 %reshape.170 = f32[4,384,256]{2,1,0:T(8,128)S(1)} reshape(f32[8,16,12,256]{3,2,1,0:T(8,128)} %copy_bitcast_fusion) | data formatting | bytes 3145728 | tf_op jit(solution)/shard_map/convert_element_type | solution.py:74
  67.5 0.2 multiply_convert_fusion.3
  67.7 5.8 %collective-permute-start.3 = (bf16[4,384,256]{2,1,0:T(8,128)(2,1)S(1)}, bf16[4,384,256]{2,1,0:T(8,128)(2,1)S(1)}, u32[]{:S(2)}, u32[]{:S(2)}) collective-permute-start(bf16[4,384,256]{2,1,0:T(8,128)(2,1)S(1)} %multiply_convert_fusion.3), channel_id=1, source_target_pairs={{48,0},{64,16},{80,32},{96,48},{112,64},{128,80},{144,96},{160,112... | collective-permute-start | bytes 2359304 | tf_op jit(solution)/shard_map/ppermute | solution.py:24
  73.5 4.2 %collective-permute-start.2 = (bf16[4,384,256]{2,1,0:T(8,128)(2,1)S(1)}, bf16[4,384,256]{2,1,0:T(8,128)(2,1)S(1)}, u32[]{:S(2)}, u32[]{:S(2)}) collective-permute-start(bf16[4,384,256]{2,1,0:T(8,128)(2,1)S(1)} %multiply_convert_fusion.3), channel_id=1, source_target_pairs={{32,0},{48,16},{64,32},{80,48},{96,64},{112,80},{128,96},{144,112}... | collective-permute-start | bytes 2359304 | tf_op jit(solution)/shard_map/ppermute | solution.py:24
  77.7 1.9 %collective-permute-start.1 = (bf16[4,384,256]{2,1,0:T(8,128)(2,1)S(1)}, bf16[4,384,256]{2,1,0:T(8,128)(2,1)S(1)}, u32[]{:S(2)}, u32[]{:S(2)}) collective-permute-start(bf16[4,384,256]{2,1,0:T(8,128)(2,1)S(1)} %multiply_convert_fusion.3), channel_id=1, source_target_pairs={{16,0},{32,16},{48,32},{64,48},{80,64},{96,80},{112,96},{128,112},... | collective-permute-start | bytes 2359304 | tf_op jit(solution)/shard_map/ppermute | solution.py:24
  79.7 8.6 %collective-permute-done.3 = bf16[4,384,256]{2,1,0:T(8,128)(2,1)S(1)} collective-permute-done((bf16[4,384,256]{2,1,0:T(8,128)(2,1)S(1)}, bf16[4,384,256]{2,1,0:T(8,128)(2,1)S(1)}, u32[]{:S(2)}, u32[]{:S(2)}) %collective-permute-start.3) | collective-permute-done | bytes 786464 | tf_op jit(solution)/shard_map/ppermute | solution.py:24
  88.3 24.4 %collective-permute-done.2 = bf16[4,384,256]{2,1,0:T(8,128)(2,1)S(1)} collective-permute-done((bf16[4,384,256]{2,1,0:T(8,128)(2,1)S(1)}, bf16[4,384,256]{2,1,0:T(8,128)(2,1)S(1)}, u32[]{:S(2)}, u32[]{:S(2)}) %collective-permute-start.2) | collective-permute-done | bytes 786464 | tf_op jit(solution)/shard_map/ppermute | solution.py:24
  112.8 6.3 %collective-permute-done.1 = bf16[4,384,256]{2,1,0:T(8,128)(2,1)S(1)} collective-permute-done((bf16[4,384,256]{2,1,0:T(8,128)(2,1)S(1)}, bf16[4,384,256]{2,1,0:T(8,128)(2,1)S(1)}, u32[]{:S(2)}, u32[]{:S(2)}) %collective-permute-start.1) | collective-permute-done | bytes 786464 | tf_op jit(solution)/shard_map/ppermute | solution.py:24
  119.1 0.8 fusion.31
  119.9 0.8 fusion.28
  120.6 0.8 fusion.25
  121.4 2.0 %pad_maximum_fusion = bf16[3,4,256,512]{3,2,1,0:T(8,128)(2,1)} fusion(bf16[1,4,256,512]{3,2,1,0:T(8,128)(2,1)S(1)} %fusion.31, bf16[1,4,256,512]{3,2,1,0:T(8,128)(2,1)S(1)} %fusion.28, bf16[1,4,256,512]{3,2,1,0:T(8,128)(2,1)S(1)} %fusion.25), kind=kLoop, calls=%fused_computation.1 | loop fusion | flops 3145728 | bytes 6291456 | tf_op jit(solution)/shard_map/stack | solution.py:83
  (17 shorter events, 0.4 us)
Async XLA Ops:
  0.0 1.5 %copy-start = (bf16[256,3072]{1,0:T(8,128)(2,1)S(1)}, bf16[256,3072]{1,0:T(8,128)(2,1)}, u32[]{:S(2)}) copy-start(bf16[256,3072]{1,0:T(8,128)(2,1)} %param.3) | copy-start | bytes 4718596
  4.2 3.0 %copy-start.2 = (s32[64]{0:T(128)S(1)}, s32[64]{0:T(128)}, u32[]{:S(2)}) copy-start(s32[64]{0:T(128)} %param.5) | copy-start | bytes 772
  5.9 12.0 %collective-permute-start = (bf16[256,768]{1,0:T(8,128)(2,1)S(1)}, bf16[256,768]{1,0:T(8,128)(2,1)}, u32[]{:S(2)}, u32[]{:S(2)}) collective-permute-start(bf16[256,768]{1,0:T(8,128)(2,1)S(1)} %slice.67), channel_id=1, source_target_pairs={{1,0},{2,1},{3,2},{4,3},{5,4},{6,5},{7,6},{8,7},{9,8},{10,9},{11,1... | collective-permute-start | bytes 1179656 | tf_op jit(solution)/shard_map/ppermute | solution.py:18
  22.9 1.3 %copy-start.1 = (bf16[1024,128]{0,1:T(8,128)(2,1)S(1)}, bf16[1024,128]{0,1:T(8,128)(2,1)}, u32[]{:S(2)}) copy-start(bf16[1024,128]{0,1:T(8,128)(2,1)} %multiply_convert_fusion.4) | copy-start | bytes 786436
  67.7 20.5 %collective-permute-start.3 = (bf16[4,384,256]{2,1,0:T(8,128)(2,1)S(1)}, bf16[4,384,256]{2,1,0:T(8,128)(2,1)S(1)}, u32[]{:S(2)}, u32[]{:S(2)}) collective-permute-start(bf16[4,384,256]{2,1,0:T(8,128)(2,1)S(1)} %multiply_convert_fusion.3), channel_id=1, source_target_pairs={{48,0},{64,16},{80,32},{96,48},{112,64},{128,80},{144,96},{160,112... | collective-permute-start | bytes 2359304 | tf_op jit(solution)/shard_map/ppermute | solution.py:24
  73.5 39.3 %collective-permute-start.2 = (bf16[4,384,256]{2,1,0:T(8,128)(2,1)S(1)}, bf16[4,384,256]{2,1,0:T(8,128)(2,1)S(1)}, u32[]{:S(2)}, u32[]{:S(2)}) collective-permute-start(bf16[4,384,256]{2,1,0:T(8,128)(2,1)S(1)} %multiply_convert_fusion.3), channel_id=1, source_target_pairs={{32,0},{48,16},{64,32},{80,48},{96,64},{112,80},{128,96},{144,112}... | collective-permute-start | bytes 2359304 | tf_op jit(solution)/shard_map/ppermute | solution.py:24
  77.7 41.3 %collective-permute-start.1 = (bf16[4,384,256]{2,1,0:T(8,128)(2,1)S(1)}, bf16[4,384,256]{2,1,0:T(8,128)(2,1)S(1)}, u32[]{:S(2)}, u32[]{:S(2)}) collective-permute-start(bf16[4,384,256]{2,1,0:T(8,128)(2,1)S(1)} %multiply_convert_fusion.3), channel_id=1, source_target_pairs={{16,0},{32,16},{48,32},{64,48},{80,64},{96,80},{112,96},{128,112},... | collective-permute-start | bytes 2359304 | tf_op jit(solution)/shard_map/ppermute | solution.py:24
where the time goes:
time: 124 us; the launch traced here: 123 us
  waiting for transfers between devices  43.6 us (35%)
  blocking collectives  37.6 us (30%)
  starting transfers between devices  13.2 us (11%)
  other arithmetic  13 us (10%)
  local copies, waits for them, and re-layouts  10.9 us (9%)
  matrix products  4.89 us (4%)
    ppermute x3, waiting for transfers between devices, from_behind_2(): return lax.ppermute(block, axis, route)  39.3 us
    all_to_all x1, blocking collectives, local(): lax.all_to_all(rounded, 'span', split_axis=0, concat_axis=1, tiled=True)  37.6 us
    ppermute x3, starting transfers between devices, from_behind_2(): return lax.ppermute(block, axis, route)  11.9 us
    ppermute x1, waiting for transfers between devices, from_behind(): return lax.ppermute(x, axis, pairs)  4.3 us
    another operation x2, local copies, waits for them, and re-layouts, dft_table(): cos_sin = jnp.stack([jnp.cos(angles), -jnp.sin(angles)], axis=-1)  3.39 us
    gather x1, local copies, waits for them, and re-layouts, local(): ordered = jnp.take(strain, channel_map[0], axis=0)  2.7 us
    concatenate x1, local copies, waits for them, and re-layouts, local(): jnp.concatenate([ordered, next_tail], axis=1)  2.67 us
    dot_general x4, matrix products, local(): jnp.einsum('chs,sk->khc', extended[:, quarter:quarter + win_local], fouri...  2.62 us
  transfers between devices with their start and end apart: 4, of which 4 were waited for; matrix products, arithmetic and copies ran while one was open for 5% of the time, Pallas kernels for 0%

commit v1 on v0

v1 whole, which is shorter than its diff:
```python
import functools
import math

import jax
import jax.numpy as jnp
from jax import lax
from jax.experimental import pallas as pl
from jax.experimental.pallas import tpu as pltpu
from jax.sharding import PartitionSpec as P

W = 1024
HOP = W // 4
ROUNDS = 3
epsilon = 1e-06
MESH = pl.DeviceIdType.MESH
BF = jnp.bfloat16
F32 = jnp.float32

PART_WINDOWS = (8, 4)
CHUNKS = ((0, 0, 2), (0, 2, 2), (1, 0, 4))


def sin_cos(x):
    x2 = x * x
    s = x * (1.0 + x2 * (-1.0 / 6 + x2 * (1.0 / 120 + x2 * (-1.0 / 5040 + x2 * (1.0 / 362880)))))
    c = 1.0 + x2 * (-0.5 + x2 * (1.0 / 24 + x2 * (-1.0 / 720 + x2 * (1.0 / 40320 - x2 * (1.0 / 3628800)))))
    return s, c


def turned(e, s, c):
    odd = (e & 1) == 1
    cos_sign = jnp.where(((e + 1) & 2) == 0, 1.0, -1.0)
    sin_sign = jnp.where((e & 2) == 0, 1.0, -1.0)
    return jnp.where(odd, s, c) * cos_sign, jnp.where(odd, c, s) * sin_sign


def fill_basis(bin_ref, basis):
    nb = bin_ref.shape[1]
    row = lax.broadcasted_iota(jnp.int32, (nb, nb), 0)
    col = lax.broadcasted_iota(jnp.int32, (nb, nb), 1)
    bins = jnp.where(row == col, jnp.broadcast_to(bin_ref[...].astype(F32), (nb, nb)), 0.0)
    bins = jnp.sum(bins, axis=1, keepdims=True).astype(jnp.int32)
    t = lax.broadcasted_iota(jnp.int32, (nb, HOP), 1)
    bins = jnp.broadcast_to(bins, (nb, HOP))

    def parts(m):
        k = (m + 128) >> 8
        s, c = sin_cos((m - (k << 8)).astype(F32) * (2.0 * math.pi / W))
        return k, s, c

    k, s, c = parts((t * bins) & (W - 1))
    tk, ts, tc = parts(lax.broadcasted_iota(jnp.int32, (8, HOP), 1))
    for q in range(4):
        cq, sq = turned((k + q * bins) & 3, s, c)
        tq, _ = turned((tk + q) & 3, ts, tc)
        taper = (0.5 - 0.5 * tq)[:1]
        base = q * 2 * nb
        basis[base : base + nb] = (taper * cq).astype(BF)
        basis[base + nb : base + 2 * nb] = (-taper * sq).astype(BF)


def exchange(
    nz, ngrp, map_ref, bin_ref, strain_ref, slab_a, slab_b,
    basis, onehot, wacc, rows_a, rows_b, out_a, out_b, transit_a, transit_b, halo_out, halo_in,
    halo_send, halo_recv, z_send, z_recv, t_recv, x_send, m_recv, x_recv, l_send, l_recv,
):
    slabs, outs, transits = (slab_a, slab_b), (out_a, out_b), (transit_a, transit_b)
    nspan = 2 * nz
    g, s = lax.axis_index("grp"), lax.axis_index("span")
    z, lo, core = s // 2, s % 2, g % 2
    nb = bin_ref.shape[1]
    channels = strain_ref.shape[0]
    win = strain_ref.shape[1] // HOP

    def at(dg, ds):
        return {"grp": lax.rem(g + dg + ngrp, ngrp), "span": ds}

    behind = lax.rem(s + nspan - 1, nspan)
    ahead = lax.rem(s + 1, nspan)
    other = z * 2 + 1 - lo

    barrier = pltpu.get_barrier_semaphore()

    def hello(device):
        pl.semaphore_signal(barrier, inc=1, device_id=device, device_id_type=MESH)

    hello(at(0, ahead))
    hello(at(0, other))
    hello(at(2, s))
    hello(at(2, other))
    hello(at(1 + 2 * core, s))
    hello(at(1 - 2 * core, s))

    def hello_z(d, _):
        hello(at(0, lax.rem(z + d, nz) * 2 + lo))
        return 0

    lax.fori_loop(1, nz, hello_z, 0)

    fill_basis(bin_ref, basis)
    c_in = lax.broadcasted_iota(jnp.int32, (channels, channels), 0)
    onehot[...] = jnp.where(c_in == jnp.broadcast_to(map_ref[...], (channels, channels)), 1.0, 0.0).astype(BF)

    def hop(j):
        block = strain_ref[:, j * HOP : (j + 1) * HOP]
        part = lax.dot_general(
            basis[...], block, (((1,), (1,)), ((), ())), preferred_element_type=F32
        )
        for q in range(4):
            i = j - q + 3
            piece = part[q * 2 * nb : (q + 1) * 2 * nb]
            if j == 0 or q == 0:
                wacc[i] = piece
            else:
                wacc[i] = wacc[i] + piece

    for j in range(3):
        hop(j)
    halo_out[...] = wacc[0:3].astype(BF)
    pl.semaphore_wait(barrier, nz - 1 + 6)
    halo = pltpu.make_async_remote_copy(
        src_ref=halo_out, dst_ref=halo_in, send_sem=halo_send, recv_sem=halo_recv,
        device_id=at(0, behind), device_id_type=MESH,
    )
    halo.start()
    for j in range(3, win):
        hop(j)

    def arrange(part, first):
        rows, out = (rows_a, rows_b)[part], outs[part]
        per = 2 * PART_WINDOWS[part]
        for w in range(PART_WINDOWS[part]):
            for p in range(2):
                at_row = (w // 4) * 8 + p * 4 + w % 4
                piece = wacc[3 + first + w, p * nb : (p + 1) * nb, :]
                for h in range(channels // 128):
                    rows[h, pl.ds(at_row, nb, stride=per), :] = piece[:, h * 128 : (h + 1) * 128]
        by_map = jnp.concatenate([rows[h].astype(BF) for h in range(channels // 128)], axis=1)
        ordered = jnp.dot(by_map, onehot[...], preferred_element_type=F32)
        out[...] = ordered.reshape(out.shape).astype(BF)

    def to_slabs(c):
        part, n0, nn = CHUNKS[c]
        out, slab, transit = outs[part], slabs[part], transits[part]
        n = pl.ds(n0, nn)
        pltpu.make_async_copy(out.at[z, 1 - lo, n], transit.at[n, z], t_recv.at[c]).start()
        pltpu.make_async_copy(out.at[z, lo, n], slab.at[0, lo, n, z], z_recv.at[c]).start()

        def send(i, _):
            off = (i + 1) // 2
            there = lax.rem(z + nz // 2 + off * (1 - 2 * (i % 2)), nz)
            device = at(0, there * 2 + lo)
            pltpu.make_async_remote_copy(
                src_ref=out.at[there, 1 - lo, n], dst_ref=transit.at[n, z],
                send_sem=z_send.at[part], recv_sem=t_recv.at[c],
                device_id=device, device_id_type=MESH,
            ).start()
            pltpu.make_async_remote_copy(
                src_ref=out.at[there, lo, n], dst_ref=slab.at[0, lo, n, z],
                send_sem=z_send.at[part], recv_sem=z_recv.at[c],
                device_id=device, device_id_type=MESH,
            ).start()
            return 0

        lax.fori_loop(0, nz - 1, send, 0)

    def arrived(ref, sem):
        pltpu.make_async_copy(ref, ref, sem).wait()

    sent = []

    def send(src, dst, send_sem, recv_sem, device):
        copy = pltpu.make_async_remote_copy(
            src_ref=src, dst_ref=dst, send_sem=send_sem, recv_sem=recv_sem,
            device_id=device, device_id_type=MESH,
        )
        copy.start()
        sent.append(copy)

    def across(c):
        part, n0, nn = CHUNKS[c]
        slab, transit = slabs[part], transits[part]
        n = pl.ds(n0, nn)
        arrived(transit.at[n], t_recv.at[c])
        send(transit.at[n], slab.at[0, lo, n], x_send.at[c, 0], m_recv.at[c], at(0, other))
        send(transit.at[n], slab.at[2, lo, n], x_send.at[c, 1], x_recv.at[c], at(-2, other))
        arrived(slab.at[0, lo, n], z_recv.at[c])
        send(slab.at[0, lo, n], slab.at[2, lo, n], x_send.at[c, 2], x_recv.at[c], at(-2, s))

    def onward(c):
        part, n0, nn = CHUNKS[c]
        slab = slabs[part]
        n = pl.ds(n0, nn)
        arrived(slab.at[0, 1 - lo, n], m_recv.at[c])
        to = 3 - 2 * core
        send(slab.at[0, :, n], slab.at[to, :, n], l_send.at[c, 0], l_recv.at[c, to // 2], at(-to, s))
        arrived(slab.at[2, :, n], x_recv.at[c])
        to = 1 + 2 * core
        send(slab.at[2, :, n], slab.at[to, :, n], l_send.at[c, 1], l_recv.at[c, to // 2], at(2 - to, s))

    def last(c):
        part, n0, nn = CHUNKS[c]
        slab = slabs[part]
        n = pl.ds(n0, nn)
        arrived(slab.at[1, :, n], l_recv.at[c, 0])
        arrived(slab.at[3, :, n], l_recv.at[c, 1])

    arrange(0, 0)
    to_slabs(0)
    to_slabs(1)
    halo.wait()
    keep = jnp.where(s == nspan - 1, 0.0, 1.0)
    for i in range(3):
        wacc[win + i] = wacc[win + i] + halo_in[i].astype(F32) * keep
    arrange(1, PART_WINDOWS[0])
    to_slabs(2)
    for c in range(len(CHUNKS)):
        across(c)
        if c:
            onward(c - 1)
    onward(len(CHUNKS) - 1)
    for c in range(len(CHUNKS)):
        last(c)
    for part in range(2):
        arrived(outs[part].at[pl.ds(0, nz - 1)], z_send.at[part])
    for copy in sent:
        copy.wait_send()


def stacked(scale, a_ref, b_ref, o_ref):
    def whitened(slot):
        a = a_ref[slot, :, 0].astype(F32)
        b = b_ref[slot, :, 0].astype(F32)
        ch = a.shape[-1]
        v = jnp.concatenate([a.reshape(-1, ch), b.reshape(-1, ch)], axis=0)
        power = jnp.sum(v * v, axis=0, keepdims=True) * (1.0 / v.shape[0])
        return v * lax.rsqrt(power + epsilon)

    own = whitened(0).astype(BF).astype(F32)
    k, ch = own.shape
    swapped = pltpu.roll(own.reshape(k // 8, 8, ch), 4, 1)
    imag_row = lax.broadcasted_iota(jnp.int32, swapped.shape, 1) >= 4
    swapped = jnp.where(imag_row, -swapped, swapped).reshape(k, ch)
    left = jnp.concatenate([own, swapped], axis=1).astype(BF)
    for r in range(ROUNDS):
        right = whitened(1 + r).astype(BF)
        both = lax.dot_general(left, right, (((0,), (0,)), ((), ())), preferred_element_type=F32)
        both = (both * scale).astype(BF)
        o_ref[r, 0, :, :ch] = both[:ch]
        o_ref[r, 0, :, ch:] = both[ch:]


def local(strain, channel_map, bin_index):
    channels = strain.shape[0]
    nspan, ngrp = lax.axis_size("span"), lax.axis_size("grp")
    nz = nspan // 2
    nb = bin_index.shape[0]
    per = nb // nspan
    rows = [2 * w for w in PART_WINDOWS]
    win = sum(PART_WINDOWS)
    nc = len(CHUNKS)
    dma = pltpu.SemaphoreType.DMA
    vmem = pl.BlockSpec(memory_space=pltpu.VMEM)
    slabs = pl.pallas_call(
        functools.partial(exchange, nz, ngrp),
        out_shape=[jax.ShapeDtypeStruct((ROUNDS + 1, 2, per, nz, r, channels), BF) for r in rows],
        in_specs=[vmem] * 3,
        out_specs=[pl.BlockSpec(memory_space=pl.ANY)] * 2,
        scratch_shapes=[
            pltpu.VMEM((8 * nb, HOP), BF),
            pltpu.VMEM((channels, channels), BF),
            pltpu.VMEM((win + 3, 2 * nb, channels), F32),
            pltpu.VMEM((channels // 128, nb * rows[0], 128), F32),
            pltpu.VMEM((channels // 128, nb * rows[1], 128), F32),
            pltpu.VMEM((nz, 2, per, rows[0], channels), BF),
            pltpu.VMEM((nz, 2, per, rows[1], channels), BF),
            pltpu.VMEM((per, nz, rows[0], channels), BF),
            pltpu.VMEM((per, nz, rows[1], channels), BF),
            pltpu.VMEM((3, 2 * nb, channels), BF),
            pltpu.VMEM((3, 2 * nb, channels), BF),
            dma, dma, dma((2,)), dma((nc,)), dma((nc,)), dma((nc, 3)), dma((nc,)), dma((nc,)), dma((nc, 2)), dma((nc, 2)),
        ],
        compiler_params=pltpu.CompilerParams(
            collective_id=0, has_side_effects=True, vmem_limit_bytes=32 * 2**20
        ),
        name="exchange",
    )(channel_map, bin_index.reshape(1, nb), strain)

    def block(r):
        return pl.BlockSpec((ROUNDS + 1, 2, 1, nz, r, channels), lambda i: (0, 0, i, 0, 0, 0))

    return pl.pallas_call(
        functools.partial(stacked, 1.0 / math.sqrt(win * nspan)),
        grid=(per,),
        in_specs=[block(r) for r in rows],
        out_specs=pl.BlockSpec((ROUNDS, 1, channels, 2 * channels), lambda i: (0, i, 0, 0)),
        out_shape=jax.ShapeDtypeStruct((ROUNDS, per, channels, 2 * channels), BF),
        compiler_params=pltpu.CompilerParams(vmem_limit_bytes=32 * 2**20),
        name="stacked",
    )(*slabs)


def solution(mesh):
    return jax.shard_map(
        local,
        mesh=mesh,
        in_specs=(P("grp", "span"), P("grp", None), P()),
        out_specs=P(None, "span", "grp", None),
        check_vma=False,
    )
```

time: 124 us -> 57.4 us (0.46)
  the two profiles are of different devices: /device:TPU:29 before, /device:TPU:89 now
where the time goes in v1:
time: 57.4 us; the launch traced here: 57.2 us
  Pallas kernels  54.4 us (95%)
  local copies, waits for them, and re-layouts  2.74 us (5%)
    pallas_call x1, Pallas kernels, local(): pl.pallas_call(functools.partial(exchange, nz, ngrp), out_shape=[jax.Shap...  50.3 us
    pallas_call x1, Pallas kernels, local(): pl.pallas_call(functools.partial(stacked, 1.0 / math.sqrt(win * nspan)),...  4.19 us
    unnamed x6, local copies, waits for them, and re-layouts  2.74 us

profile of v1, /device:TPU:89, one launch (start us, length us, event | category | flops | bytes accessed | tf_op | source)
XLA Modules:
  0.0 57.2 jit_solution(16691700134444863464)
XLA Ops:
  0.0 0.0 copy-start
  0.0 1.4 %copy-done = bf16[256,3072]{1,0:T(8,128)(2,1)S(1)} copy-done((bf16[256,3072]{1,0:T(8,128)(2,1)S(1)}, bf16[256,3072]{1,0:T(8,128)(2,1)}, u32[]{:S(2)}) %copy-start) | copy-done | bytes 1572888
  1.4 0.0 copy-start.1
  1.4 0.7 %copy-done.1 = s32[1,256]{1,0:T(1,128)S(1)} copy-done((s32[1,256]{1,0:T(1,128)S(1)}, s32[1,256]{1,0:T(1,128)}, u32[]{:S(2)}) %copy-start.1) | copy-done | bytes 1048
  2.1 0.0 copy-start.2
  2.1 0.7 %copy-done.2 = s32[64]{0:T(128)S(1)} copy-done((s32[64]{0:T(128)S(1)}, s32[64]{0:T(128)}, u32[]{:S(2)}) %copy-start.2) | copy-done | bytes 280
  2.7 50.3 %exchange.1 = (bf16[4,2,4,8,16,256]{5,4,3,2,1,0:T(8,128)(2,1)S(1)}, bf16[4,2,4,8,8,256]{5,4,3,2,1,0:T(8,128)(2,1)S(1)}) custom-call(s32[1,256]{1,0:T(1,128)S(1)} %copy-done.1, s32[1,64]{1,0:T(1,128)S(1)} %bitcast.1, bf16[256,3072]{1,0:T(8,128)(2,1)S(1)} %copy-done), custom_call_target="tpu_custom_call" | custom-call | tf_op jit(solution)/shard_map/exchange/pallas_call | solution.py:264
  53.0 4.2 %stacked.1 = bf16[3,4,256,512]{3,2,1,0:T(8,128)(2,1)} custom-call(bf16[4,2,4,8,16,256]{5,4,3,2,1,0:T(8,128)(2,1)S(1)} %get-tuple-element.7.a_ref, bf16[4,2,4,8,8,256]{5,4,3,2,1,0:T(8,128)(2,1)S(1)} %get-tuple-element.8.b_ref), custom_call_target="tpu_custom_call" | custom-call | tf_op jit(solution)/shard_map/stacked/pallas_call | solution.py:292
Async XLA Ops:
  0.0 1.4 %copy-start = (bf16[256,3072]{1,0:T(8,128)(2,1)S(1)}, bf16[256,3072]{1,0:T(8,128)(2,1)}, u32[]{:S(2)}) copy-start(bf16[256,3072]{1,0:T(8,128)(2,1)} %strain_ref.1) | copy-start | bytes 4718596
  1.4 0.7 %copy-start.1 = (s32[1,256]{1,0:T(1,128)S(1)}, s32[1,256]{1,0:T(1,128)}, u32[]{:S(2)}) copy-start(s32[1,256]{1,0:T(1,128)} %map_ref.1) | copy-start | bytes 3076
  2.1 0.7 %copy-start.2 = (s32[64]{0:T(128)S(1)}, s32[64]{0:T(128)}, u32[]{:S(2)}) copy-start(s32[64]{0:T(128)} %param.5) | copy-start | bytes 772

commit v2 on v1

--- a/solution.py
+++ b/solution.py
@@ -17,7 +17,7 @@
 F32 = jnp.float32
 
 PART_WINDOWS = (8, 4)
-CHUNKS = ((0, 0, 2), (0, 2, 2), (1, 0, 4))
+CHUNKS = ((0, 0, 1), (0, 1, 1), (0, 2, 1), (0, 3, 1), (1, 0, 2), (1, 2, 2))
 
 
 def sin_cos(x):
@@ -60,9 +60,9 @@
 
 
 def exchange(
-    nz, ngrp, map_ref, bin_ref, strain_ref, slab_a, slab_b,
-    basis, onehot, wacc, rows_a, rows_b, out_a, out_b, transit_a, transit_b, halo_out, halo_in,
-    halo_send, halo_recv, z_send, z_recv, t_recv, x_send, m_recv, x_recv, l_send, l_recv,
+    nz, ngrp, map_hbm, bin_hbm, strain_hbm, slab_a, slab_b,
+    map_ref, bin_ref, strain_ref, load_sem, basis, onehot, wacc, rows_a, rows_b, out_a, out_b, transit_a, transit_b, halo_out, halo_in,
+    halo_send, halo_recv, z_send, z_recv, t_recv, x_send, m_recv, x_recv, r_send, l_send, l_recv,
 ):
     slabs, outs, transits = (slab_a, slab_b), (out_a, out_b), (transit_a, transit_b)
     nspan = 2 * nz
@@ -72,8 +72,18 @@
     channels = strain_ref.shape[0]
     win = strain_ref.shape[1] // HOP
 
+    loads = [
+        pltpu.make_async_copy(bin_hbm, bin_ref, load_sem.at[win]),
+        pltpu.make_async_copy(map_hbm, map_ref, load_sem.at[win + 1]),
+    ]
+    for j in range(win):
+        hop_samples = (slice(None), slice(j * HOP, (j + 1) * HOP))
+        loads.append(pltpu.make_async_copy(strain_hbm.at[hop_samples], strain_ref.at[hop_samples], load_sem.at[j]))
+    for load in loads:
+        load.start()
+
     def at(dg, ds):
-        return {"grp": lax.rem(g + dg + ngrp, ngrp), "span": ds}
+        return {"grp": lax.rem(g + dg + 2 * ngrp, ngrp), "span": ds}
 
     behind = lax.rem(s + nspan - 1, nspan)
     ahead = lax.rem(s + 1, nspan)
@@ -86,8 +96,16 @@
 
     hello(at(0, ahead))
     hello(at(0, other))
-    hello(at(2, s))
-    hello(at(2, other))
+    quarter = lax.rem(g, 4)
+    relayed = jnp.where(quarter == 1, 1, 0)
+    relaying = jnp.where(quarter == 3, 1, 0)
+    hello(at(2 - 4 * relaying, s))
+    hello(at(2 - 4 * relaying, other))
+
+    @pl.when(relaying == 1)
+    def _():
+        hello(at(4, s))
+
     hello(at(1 + 2 * core, s))
     hello(at(1 - 2 * core, s))
 
@@ -97,11 +115,14 @@
 
     lax.fori_loop(1, nz, hello_z, 0)
 
+    loads[0].wait()
     fill_basis(bin_ref, basis)
+    loads[1].wait()
     c_in = lax.broadcasted_iota(jnp.int32, (channels, channels), 0)
     onehot[...] = jnp.where(c_in == jnp.broadcast_to(map_ref[...], (channels, channels)), 1.0, 0.0).astype(BF)
 
     def hop(j):
+        loads[2 + j].wait()
         block = strain_ref[:, j * HOP : (j + 1) * HOP]
         part = lax.dot_general(
             basis[...], block, (((1,), (1,)), ((), ())), preferred_element_type=F32
@@ -117,7 +138,7 @@
     for j in range(3):
         hop(j)
     halo_out[...] = wacc[0:3].astype(BF)
-    pl.semaphore_wait(barrier, nz - 1 + 6)
+    pl.semaphore_wait(barrier, nz - 1 + 6 + relaying)
     halo = pltpu.make_async_remote_copy(
         src_ref=halo_out, dst_ref=halo_in, send_sem=halo_send, recv_sem=halo_recv,
         device_id=at(0, behind), device_id_type=MESH,
@@ -146,23 +167,21 @@
         pltpu.make_async_copy(out.at[z, 1 - lo, n], transit.at[n, z], t_recv.at[c]).start()
         pltpu.make_async_copy(out.at[z, lo, n], slab.at[0, lo, n, z], z_recv.at[c]).start()
 
-        def send(i, _):
-            off = (i + 1) // 2
-            there = lax.rem(z + nz // 2 + off * (1 - 2 * (i % 2)), nz)
-            device = at(0, there * 2 + lo)
-            pltpu.make_async_remote_copy(
-                src_ref=out.at[there, 1 - lo, n], dst_ref=transit.at[n, z],
-                send_sem=z_send.at[part], recv_sem=t_recv.at[c],
-                device_id=device, device_id_type=MESH,
-            ).start()
-            pltpu.make_async_remote_copy(
-                src_ref=out.at[there, lo, n], dst_ref=slab.at[0, lo, n, z],
-                send_sem=z_send.at[part], recv_sem=z_recv.at[c],
-                device_id=device, device_id_type=MESH,
-            ).start()
-            return 0
-
-        lax.fori_loop(0, nz - 1, send, 0)
+        def send(half, recv_sem, dst):
+            def step(i, _):
+                off = (i + 1) // 2
+                there = lax.rem(z + nz // 2 + off * (1 - 2 * (i % 2)), nz)
+                pltpu.make_async_remote_copy(
+                    src_ref=out.at[there, half, n], dst_ref=dst,
+                    send_sem=z_send.at[part], recv_sem=recv_sem,
+                    device_id=at(0, there * 2 + lo), device_id_type=MESH,
+                ).start()
+                return 0
+
+            lax.fori_loop(0, nz - 1, step, 0)
+
+        send(1 - lo, t_recv.at[c], transit.at[n, z])
+        send(lo, z_recv.at[c], slab.at[0, lo, n, z])
 
     def arrived(ref, sem):
         pltpu.make_async_copy(ref, ref, sem).wait()
@@ -181,20 +200,35 @@
         part, n0, nn = CHUNKS[c]
         slab, transit = slabs[part], transits[part]
         n = pl.ds(n0, nn)
+        to, dg, sem = 2 + 2 * relayed, 4 * relayed - 2, x_recv.at[c, relayed]
         arrived(transit.at[n], t_recv.at[c])
+        send(transit.at[n], slab.at[to, lo, n], x_send.at[c, 1], sem, at(dg, other))
         send(transit.at[n], slab.at[0, lo, n], x_send.at[c, 0], m_recv.at[c], at(0, other))
-        send(transit.at[n], slab.at[2, lo, n], x_send.at[c, 1], x_recv.at[c], at(-2, other))
         arrived(slab.at[0, lo, n], z_recv.at[c])
-        send(slab.at[0, lo, n], slab.at[2, lo, n], x_send.at[c, 2], x_recv.at[c], at(-2, s))
-
-    def onward(c):
+        send(slab.at[0, lo, n], slab.at[to, lo, n], x_send.at[c, 2], sem, at(dg, s))
+
+    def own_onward(c):
         part, n0, nn = CHUNKS[c]
         slab = slabs[part]
         n = pl.ds(n0, nn)
+
+        @pl.when(relaying == 1)
+        def _():
+            arrived(slab.at[4, :, n], x_recv.at[c, 1])
+            pltpu.make_async_remote_copy(
+                src_ref=slab.at[4, :, n], dst_ref=slab.at[2, :, n],
+                send_sem=r_send.at[c], recv_sem=x_recv.at[c, 0], device_id=at(-4, s), device_id_type=MESH,
+            ).start()
+
         arrived(slab.at[0, 1 - lo, n], m_recv.at[c])
         to = 3 - 2 * core
         send(slab.at[0, :, n], slab.at[to, :, n], l_send.at[c, 0], l_recv.at[c, to // 2], at(-to, s))
-        arrived(slab.at[2, :, n], x_recv.at[c])
+
+    def next_onward(c):
+        part, n0, nn = CHUNKS[c]
+        slab = slabs[part]
+        n = pl.ds(n0, nn)
+        arrived(slab.at[2, :, n], x_recv.at[c, 0])
         to = 1 + 2 * core
         send(slab.at[2, :, n], slab.at[to, :, n], l_send.at[c, 1], l_recv.at[c, to // 2], at(2 - to, s))
 
@@ -206,25 +240,36 @@
         arrived(slab.at[3, :, n], l_recv.at[c, 1])
 
     arrange(0, 0)
-    to_slabs(0)
-    to_slabs(1)
+    for c in range(4):
+        to_slabs(c)
     halo.wait()
     keep = jnp.where(s == nspan - 1, 0.0, 1.0)
     for i in range(3):
         wacc[win + i] = wacc[win + i] + halo_in[i].astype(F32) * keep
     arrange(1, PART_WINDOWS[0])
-    to_slabs(2)
-    for c in range(len(CHUNKS)):
-        across(c)
-        if c:
-            onward(c - 1)
-    onward(len(CHUNKS) - 1)
-    for c in range(len(CHUNKS)):
+    nc = len(CHUNKS)
+    for c in range(4, nc):
+        to_slabs(c)
+    for c in range(nc + 2):
+        if c < nc:
+            across(c)
+        if 1 <= c <= nc:
+            own_onward(c - 1)
+        if c >= 2:
+            next_onward(c - 2)
+    for c in range(nc):
         last(c)
     for part in range(2):
         arrived(outs[part].at[pl.ds(0, nz - 1)], z_send.at[part])
     for copy in sent:
         copy.wait_send()
+
+    @pl.when(relaying == 1)
+    def _():
+        for c in range(nc):
+            part, n0, nn = CHUNKS[c]
+            ref = slabs[part].at[4, :, pl.ds(n0, nn)]
+            arrived(ref, r_send.at[c])
 
 
 def stacked(scale, a_ref, b_ref, o_ref):
@@ -260,13 +305,16 @@
     win = sum(PART_WINDOWS)
     nc = len(CHUNKS)
     dma = pltpu.SemaphoreType.DMA
-    vmem = pl.BlockSpec(memory_space=pltpu.VMEM)
     slabs = pl.pallas_call(
         functools.partial(exchange, nz, ngrp),
-        out_shape=[jax.ShapeDtypeStruct((ROUNDS + 1, 2, per, nz, r, channels), BF) for r in rows],
-        in_specs=[vmem] * 3,
+        out_shape=[jax.ShapeDtypeStruct((ROUNDS + 2, 2, per, nz, r, channels), BF) for r in rows],
+        in_specs=[pl.BlockSpec(memory_space=pltpu.HBM)] * 3,
         out_specs=[pl.BlockSpec(memory_space=pl.ANY)] * 2,
         scratch_shapes=[
+            pltpu.VMEM((1, channels), jnp.int32),
+            pltpu.VMEM((1, nb), jnp.int32),
+            pltpu.VMEM((channels, strain.shape[1]), BF),
+            dma((win + 2,)),
             pltpu.VMEM((8 * nb, HOP), BF),
             pltpu.VMEM((channels, channels), BF),
             pltpu.VMEM((win + 3, 2 * nb, channels), F32),
@@ -278,7 +326,7 @@
             pltpu.VMEM((per, nz, rows[1], channels), BF),
             pltpu.VMEM((3, 2 * nb, channels), BF),
             pltpu.VMEM((3, 2 * nb, channels), BF),
-            dma, dma, dma((2,)), dma((nc,)), dma((nc,)), dma((nc, 3)), dma((nc,)), dma((nc,)), dma((nc, 2)), dma((nc, 2)),
+            dma, dma, dma((2,)), dma((nc,)), dma((nc,)), dma((nc, 3)), dma((nc,)), dma((nc, 2)), dma((nc,)), dma((nc, 2)), dma((nc, 2)),
         ],
         compiler_params=pltpu.CompilerParams(
             collective_id=0, has_side_effects=True, vmem_limit_bytes=32 * 2**20

time: 57.4 us -> 52.5 us (0.915)
  the two profiles are of different devices: /device:TPU:89 before, /device:TPU:31 now
where the time goes in v2:
time: 52.5 us; the launch traced here: 52.3 us
  Pallas kernels  49.6 us (94%)
  local copies, waits for them, and re-layouts  2.74 us (5%)
    pallas_call x1, Pallas kernels, local(): pl.pallas_call(functools.partial(exchange, nz, ngrp), out_shape=[jax.Shap...  45.4 us
    pallas_call x1, Pallas kernels, local(): pl.pallas_call(functools.partial(stacked, 1.0 / math.sqrt(win * nspan)),...  4.19 us
    unnamed x6, local copies, waits for them, and re-layouts  2.74 us

profile of v2, /device:TPU:31, one launch (start us, length us, event | category | flops | bytes accessed | tf_op | source)
XLA Modules:
  0.0 52.3 jit_solution(2535039110824313011)
XLA Ops:
  0.0 0.0 copy-start
  0.0 1.4 %copy-done = bf16[256,3072]{1,0:T(8,128)(2,1)S(1)} copy-done((bf16[256,3072]{1,0:T(8,128)(2,1)S(1)}, bf16[256,3072]{1,0:T(8,128)(2,1)}, u32[]{:S(2)}) %copy-start) | copy-done | bytes 1572888
  1.4 0.0 copy-start.1
  1.4 0.7 %copy-done.1 = s32[1,256]{1,0:T(1,128)S(1)} copy-done((s32[1,256]{1,0:T(1,128)S(1)}, s32[1,256]{1,0:T(1,128)}, u32[]{:S(2)}) %copy-start.1) | copy-done | bytes 1048
  2.1 0.0 copy-start.2
  2.1 0.7 %copy-done.2 = s32[64]{0:T(128)S(1)} copy-done((s32[64]{0:T(128)S(1)}, s32[64]{0:T(128)}, u32[]{:S(2)}) %copy-start.2) | copy-done | bytes 280
  2.7 45.4 %exchange.1 = (bf16[5,2,4,8,16,256]{5,4,3,2,1,0:T(8,128)(2,1)S(1)}, bf16[5,2,4,8,8,256]{5,4,3,2,1,0:T(8,128)(2,1)S(1)}) custom-call(s32[1,256]{1,0:T(1,128)S(1)} %copy-done.1, s32[1,64]{1,0:T(1,128)S(1)} %bitcast.1, bf16[256,3072]{1,0:T(8,128)(2,1)S(1)} %copy-done), custom_call_target="tpu_custom_call" | custom-call | tf_op jit(solution)/shard_map/exchange/pallas_call | solution.py:308
  48.1 4.2 %stacked.1 = bf16[3,4,256,512]{3,2,1,0:T(8,128)(2,1)} custom-call(bf16[5,2,4,8,16,256]{5,4,3,2,1,0:T(8,128)(2,1)S(1)} %get-tuple-element.7.a_ref, bf16[5,2,4,8,8,256]{5,4,3,2,1,0:T(8,128)(2,1)S(1)} %get-tuple-element.8.b_ref), custom_call_target="tpu_custom_call" | custom-call | tf_op jit(solution)/shard_map/stacked/pallas_call | solution.py:340
Async XLA Ops:
  0.0 1.4 %copy-start = (bf16[256,3072]{1,0:T(8,128)(2,1)S(1)}, bf16[256,3072]{1,0:T(8,128)(2,1)}, u32[]{:S(2)}) copy-start(bf16[256,3072]{1,0:T(8,128)(2,1)} %strain_hbm.1) | copy-start | bytes 4718596
  1.4 0.7 %copy-start.1 = (s32[1,256]{1,0:T(1,128)S(1)}, s32[1,256]{1,0:T(1,128)}, u32[]{:S(2)}) copy-start(s32[1,256]{1,0:T(1,128)} %map_hbm.1) | copy-start | bytes 3076
  2.1 0.7 %copy-start.2 = (s32[64]{0:T(128)S(1)}, s32[64]{0:T(128)}, u32[]{:S(2)}) copy-start(s32[64]{0:T(128)} %param.5) | copy-start | bytes 772

commit v3 on v2

--- a/solution.py
+++ b/solution.py
@@ -17,7 +17,7 @@
 F32 = jnp.float32
 
 PART_WINDOWS = (8, 4)
-CHUNKS = ((0, 0, 1), (0, 1, 1), (0, 2, 1), (0, 3, 1), (1, 0, 2), (1, 2, 2))
+CHUNKS = ((0, 0, 1), (0, 1, 1), (1, 0, 2), (0, 2, 1), (0, 3, 1), (1, 2, 2))
 
 
 def sin_cos(x):
@@ -60,9 +60,9 @@
 
 
 def exchange(
-    nz, ngrp, map_hbm, bin_hbm, strain_hbm, slab_a, slab_b,
-    map_ref, bin_ref, strain_ref, load_sem, basis, onehot, wacc, rows_a, rows_b, out_a, out_b, transit_a, transit_b, halo_out, halo_in,
-    halo_send, halo_recv, z_send, z_recv, t_recv, x_send, m_recv, x_recv, r_send, l_send, l_recv,
+    nz, ngrp, map_hbm, bin_hbm, strain_hbm, left_hbm, right_hbm,
+    slab_a, slab_b, left_ref, right_ref, map_ref, bin_ref, strain_ref, load_sem, basis, onehot, wacc, rows_a, rows_b, out_a, out_b, transit_a, transit_b, halo_out, halo_in,
+    halo_send, halo_recv, z_send, z_recv, own_sem, x_send, m_recv, x_recv, r_send, l_send, l_recv, out_sem,
 ):
     slabs, outs, transits = (slab_a, slab_b), (out_a, out_b), (transit_a, transit_b)
     nspan = 2 * nz
@@ -162,26 +162,21 @@
 
     def to_slabs(c):
         part, n0, nn = CHUNKS[c]
-        out, slab, transit = outs[part], slabs[part], transits[part]
+        out, transit = outs[part], transits[part]
         n = pl.ds(n0, nn)
-        pltpu.make_async_copy(out.at[z, 1 - lo, n], transit.at[n, z], t_recv.at[c]).start()
-        pltpu.make_async_copy(out.at[z, lo, n], slab.at[0, lo, n, z], z_recv.at[c]).start()
-
-        def send(half, recv_sem, dst):
-            def step(i, _):
-                off = (i + 1) // 2
-                there = lax.rem(z + nz // 2 + off * (1 - 2 * (i % 2)), nz)
-                pltpu.make_async_remote_copy(
-                    src_ref=out.at[there, half, n], dst_ref=dst,
-                    send_sem=z_send.at[part], recv_sem=recv_sem,
-                    device_id=at(0, there * 2 + lo), device_id_type=MESH,
-                ).start()
-                return 0
-
-            lax.fori_loop(0, nz - 1, step, 0)
-
-        send(1 - lo, t_recv.at[c], transit.at[n, z])
-        send(lo, z_recv.at[c], slab.at[0, lo, n, z])
+        pltpu.make_async_copy(out.at[z, :, n], transit.at[:, n, z], z_recv.at[c]).start()
+
+        def step(i, _):
+            off = (i + 1) // 2
+            there = lax.rem(z + nz // 2 + off * (1 - 2 * (i % 2)), nz)
+            pltpu.make_async_remote_copy(
+                src_ref=out.at[there, :, n], dst_ref=transit.at[:, n, z],
+                send_sem=z_send.at[part], recv_sem=z_recv.at[c],
+                device_id=at(0, there * 2 + lo), device_id_type=MESH,
+            ).start()
+            return 0
+
+        lax.fori_loop(0, nz - 1, step, 0)
 
     def arrived(ref, sem):
         pltpu.make_async_copy(ref, ref, sem).wait()
@@ -201,11 +196,11 @@
         slab, transit = slabs[part], transits[part]
         n = pl.ds(n0, nn)
         to, dg, sem = 2 + 2 * relayed, 4 * relayed - 2, x_recv.at[c, relayed]
-        arrived(transit.at[n], t_recv.at[c])
-        send(transit.at[n], slab.at[to, lo, n], x_send.at[c, 1], sem, at(dg, other))
-        send(transit.at[n], slab.at[0, lo, n], x_send.at[c, 0], m_recv.at[c], at(0, other))
-        arrived(slab.at[0, lo, n], z_recv.at[c])
-        send(slab.at[0, lo, n], slab.at[to, lo, n], x_send.at[c, 2], sem, at(dg, s))
+        arrived(transit.at[:, n], z_recv.at[c])
+        send(transit.at[1 - lo, n], slab.at[to, lo, n], x_send.at[c, 1], sem, at(dg, other))
+        send(transit.at[1 - lo, n], slab.at[0, lo, n], x_send.at[c, 0], m_recv.at[c], at(0, other))
+        send(transit.at[lo, n], slab.at[to, lo, n], x_send.at[c, 2], sem, at(dg, s))
+        pltpu.make_async_copy(transit.at[lo, n], slab.at[0, lo, n], own_sem.at[c]).start()
 
     def own_onward(c):
         part, n0, nn = CHUNKS[c]
@@ -220,6 +215,7 @@
                 send_sem=r_send.at[c], recv_sem=x_recv.at[c, 0], device_id=at(-4, s), device_id_type=MESH,
             ).start()
 
+        arrived(slab.at[0, lo, n], own_sem.at[c])
         arrived(slab.at[0, 1 - lo, n], m_recv.at[c])
         to = 3 - 2 * core
         send(slab.at[0, :, n], slab.at[to, :, n], l_send.at[c, 0], l_recv.at[c, to // 2], at(-to, s))
@@ -239,26 +235,82 @@
         arrived(slab.at[1, :, n], l_recv.at[c, 0])
         arrived(slab.at[3, :, n], l_recv.at[c, 1])
 
+    def whitened(slot, n):
+        a = slab_a[slot, :, n].astype(F32)
+        b = slab_b[slot, :, n].astype(F32)
+        v = jnp.concatenate([a.reshape(-1, channels), b.reshape(-1, channels)], axis=0)
+        power = jnp.sum(v * v, axis=0, keepdims=True) * (1.0 / v.shape[0])
+        return (v * lax.rsqrt(power + epsilon)).astype(BF)
+
+    written = []
+
+    def put(src, dst, sem):
+        copy = pltpu.make_async_copy(src, dst, sem)
+        copy.start()
+        written.append(copy)
+
+    def own_bins(bins):
+        for n in bins:
+            own = whitened(0, n).astype(F32)
+            swapped = pltpu.roll(own.reshape(-1, 8, channels), 4, 1)
+            imag_row = lax.broadcasted_iota(jnp.int32, swapped.shape, 1) >= 4
+            swapped = jnp.where(imag_row, -swapped, swapped).reshape(own.shape)
+            left_ref[n, :channels] = own.T.astype(BF)
+            left_ref[n, channels:] = swapped.T.astype(BF)
+            put(left_ref.at[n], left_hbm.at[n], out_sem.at[0, n])
+
+    def next_bins(slot, bins):
+        for n in bins:
+            right_ref[n, slot - 1] = whitened(slot, n)
+            put(right_ref.at[n, slot - 1], right_hbm.at[n, slot - 1], out_sem.at[slot, n])
+
     arrange(0, 0)
-    for c in range(4):
-        to_slabs(c)
+    to_slabs(0)
+    to_slabs(1)
     halo.wait()
     keep = jnp.where(s == nspan - 1, 0.0, 1.0)
     for i in range(3):
         wacc[win + i] = wacc[win + i] + halo_in[i].astype(F32) * keep
     arrange(1, PART_WINDOWS[0])
+    to_slabs(2)
+    to_slabs(3)
+    across(0)
+    to_slabs(4)
+    across(1)
+    own_onward(0)
+    to_slabs(5)
+    across(2)
+    own_onward(1)
+    next_onward(0)
+    across(3)
+    own_onward(2)
+    next_onward(1)
+    own_bins((0, 1))
+    across(4)
+    own_onward(3)
+    next_onward(2)
+    last(0)
+    next_bins(2, (0, 1))
+    across(5)
+    own_onward(4)
+    next_onward(3)
+    last(1)
+    last(2)
+    next_bins(1, (0, 1))
+    next_bins(3, (0, 1))
+    own_onward(5)
+    next_onward(4)
+    own_bins((2, 3))
+    next_onward(5)
+    last(3)
+    last(4)
+    next_bins(2, (2, 3))
+    last(5)
+    next_bins(1, (2, 3))
+    next_bins(3, (2, 3))
     nc = len(CHUNKS)
-    for c in range(4, nc):
-        to_slabs(c)
-    for c in range(nc + 2):
-        if c < nc:
-            across(c)
-        if 1 <= c <= nc:
-            own_onward(c - 1)
-        if c >= 2:
-            next_onward(c - 2)
-    for c in range(nc):
-        last(c)
+    for copy in written:
+        copy.wait()
     for part in range(2):
         arrived(outs[part].at[pl.ds(0, nz - 1)], z_send.at[part])
     for copy in sent:
@@ -272,24 +324,10 @@
             arrived(ref, r_send.at[c])
 
 
-def stacked(scale, a_ref, b_ref, o_ref):
-    def whitened(slot):
-        a = a_ref[slot, :, 0].astype(F32)
-        b = b_ref[slot, :, 0].astype(F32)
-        ch = a.shape[-1]
-        v = jnp.concatenate([a.reshape(-1, ch), b.reshape(-1, ch)], axis=0)
-        power = jnp.sum(v * v, axis=0, keepdims=True) * (1.0 / v.shape[0])
-        return v * lax.rsqrt(power + epsilon)
-
-    own = whitened(0).astype(BF).astype(F32)
-    k, ch = own.shape
-    swapped = pltpu.roll(own.reshape(k // 8, 8, ch), 4, 1)
-    imag_row = lax.broadcasted_iota(jnp.int32, swapped.shape, 1) >= 4
-    swapped = jnp.where(imag_row, -swapped, swapped).reshape(k, ch)
-    left = jnp.concatenate([own, swapped], axis=1).astype(BF)
+def stacked(scale, left_ref, right_ref, o_ref):
+    ch = right_ref.shape[-1]
     for r in range(ROUNDS):
-        right = whitened(1 + r).astype(BF)
-        both = lax.dot_general(left, right, (((0,), (0,)), ((), ())), preferred_element_type=F32)
+        both = jnp.dot(left_ref[0], right_ref[0, r], preferred_element_type=F32)
         both = (both * scale).astype(BF)
         o_ref[r, 0, :, :ch] = both[:ch]
         o_ref[r, 0, :, ch:] = both[ch:]
@@ -305,12 +343,20 @@
     win = sum(PART_WINDOWS)
     nc = len(CHUNKS)
     dma = pltpu.SemaphoreType.DMA
-    slabs = pl.pallas_call(
+    depth = nspan * sum(rows)
+    left, right = pl.pallas_call(
         functools.partial(exchange, nz, ngrp),
-        out_shape=[jax.ShapeDtypeStruct((ROUNDS + 2, 2, per, nz, r, channels), BF) for r in rows],
+        out_shape=[
+            jax.ShapeDtypeStruct((per, 2 * channels, depth), BF),
+            jax.ShapeDtypeStruct((per, ROUNDS, depth, channels), BF),
+        ],
         in_specs=[pl.BlockSpec(memory_space=pltpu.HBM)] * 3,
         out_specs=[pl.BlockSpec(memory_space=pl.ANY)] * 2,
         scratch_shapes=[
+            pltpu.VMEM((ROUNDS + 2, 2, per, nz, rows[0], channels), BF),
+            pltpu.VMEM((ROUNDS + 2, 2, per, nz, rows[1], channels), BF),
+            pltpu.VMEM((per, 2 * channels, depth), BF),
+            pltpu.VMEM((per, ROUNDS, depth, channels), BF),
             pltpu.VMEM((1, channels), jnp.int32),
             pltpu.VMEM((1, nb), jnp.int32),
             pltpu.VMEM((channels, strain.shape[1]), BF),
@@ -322,30 +368,30 @@
             pltpu.VMEM((channels // 128, nb * rows[1], 128), F32),
             pltpu.VMEM((nz, 2, per, rows[0], channels), BF),
             pltpu.VMEM((nz, 2, per, rows[1], channels), BF),
-            pltpu.VMEM((per, nz, rows[0], channels), BF),
-            pltpu.VMEM((per, nz, rows[1], channels), BF),
+            pltpu.VMEM((2, per, nz, rows[0], channels), BF),
+            pltpu.VMEM((2, per, nz, rows[1], channels), BF),
             pltpu.VMEM((3, 2 * nb, channels), BF),
             pltpu.VMEM((3, 2 * nb, channels), BF),
-            dma, dma, dma((2,)), dma((nc,)), dma((nc,)), dma((nc, 3)), dma((nc,)), dma((nc, 2)), dma((nc,)), dma((nc, 2)), dma((nc, 2)),
+            dma, dma, dma((2,)), dma((nc,)), dma((nc,)), dma((nc, 3)), dma((nc,)), dma((nc, 2)), dma((nc,)), dma((nc, 2)), dma((nc, 2)), dma((ROUNDS + 1, per)),
         ],
         compiler_params=pltpu.CompilerParams(
-            collective_id=0, has_side_effects=True, vmem_limit_bytes=32 * 2**20
+            collective_id=0, has_side_effects=True, vmem_limit_bytes=58_000_000
         ),
         name="exchange",
     )(channel_map, bin_index.reshape(1, nb), strain)
 
-    def block(r):
-        return pl.BlockSpec((ROUNDS + 1, 2, 1, nz, r, channels), lambda i: (0, 0, i, 0, 0, 0))
-
     return pl.pallas_call(
         functools.partial(stacked, 1.0 / math.sqrt(win * nspan)),
         grid=(per,),
-        in_specs=[block(r) for r in rows],
+        in_specs=[
+            pl.BlockSpec((1, 2 * channels, depth), lambda i: (i, 0, 0)),
+            pl.BlockSpec((1, ROUNDS, depth, channels), lambda i: (i, 0, 0, 0)),
+        ],
         out_specs=pl.BlockSpec((ROUNDS, 1, channels, 2 * channels), lambda i: (0, i, 0, 0)),
         out_shape=jax.ShapeDtypeStruct((ROUNDS, per, channels, 2 * channels), BF),
         compiler_params=pltpu.CompilerParams(vmem_limit_bytes=32 * 2**20),
         name="stacked",
-    )(*slabs)
+    )(left, right)
 
 
 def solution(mesh):

time: 52.5 us -> 53.3 us (1.015)
    pallas_call x1, Pallas kernels: 45.4 us -> 46.5 us  [local(): pl.pallas_call(functools.partial(exchange, nz, ngrp), out_shape=[jax.Shap...]
    pallas_call x1, Pallas kernels: 4.19 us -> 3.49 us  [local(): pl.pallas_call(functools.partial(stacked, 1.0 / math.sqrt(win * nspan)),...]
    unnamed x6 -> x4, local copies, waits for them, and re-layouts: 2.74 us -> 3.07 us
where the time goes in v3:
time: 53.3 us; the launch traced here: 53.1 us
  Pallas kernels  50 us (94%)
  local copies, waits for them, and re-layouts  3.07 us (6%)
    pallas_call x1, Pallas kernels, local(): pl.pallas_call(functools.partial(exchange, nz, ngrp), out_shape=[jax.Shap...  46.5 us
    pallas_call x1, Pallas kernels, local(): pl.pallas_call(functools.partial(stacked, 1.0 / math.sqrt(win * nspan)),...  3.49 us
    unnamed x4, local copies, waits for them, and re-layouts  3.07 us

profile of v3, /device:TPU:31, one launch (start us, length us, event | category | flops | bytes accessed | tf_op | source)
XLA Modules:
  0.0 53.1 jit_solution(13364549083548853703)
XLA Ops:
  0.0 46.5 %exchange.1 = (bf16[4,512,384]{2,1,0:T(8,128)(2,1)}, bf16[4,3,384,256]{3,2,1,0:T(8,128)(2,1)}) custom-call(s32[1,256]{1,0:T(1,128)} %map_hbm.1, s32[1,64]{1,0:T(1,128)} %bitcast.1, bf16[256,3072]{1,0:T(8,128)(2,1)} %strain_hbm.1), custom_call_target="tpu_custom_call" | custom-call | tf_op jit(solution)/shard_map/exchange/pallas_call | solution.py:347
  46.5 0.0 copy-start
  46.5 1.7 %copy-done = bf16[4,3,384,256]{3,2,1,0:T(8,128)(2,1)S(1)} copy-done((bf16[4,3,384,256]{3,2,1,0:T(8,128)(2,1)S(1)}, bf16[4,3,384,256]{3,2,1,0:T(8,128)(2,1)}, u32[]{:S(2)}) %copy-start) | copy-done | bytes 2359320
  48.2 0.0 copy-start.1
  48.2 1.4 %copy-done.1 = bf16[4,512,384]{2,1,0:T(8,128)(2,1)S(1)} copy-done((bf16[4,512,384]{2,1,0:T(8,128)(2,1)S(1)}, bf16[4,512,384]{2,1,0:T(8,128)(2,1)}, u32[]{:S(2)}) %copy-start.1) | copy-done | bytes 1572888
  49.6 3.5 %stacked.1 = bf16[3,4,256,512]{3,2,1,0:T(8,128)(2,1)} custom-call(bf16[4,512,384]{2,1,0:T(8,128)(2,1)S(1)} %copy-done.1, bf16[4,3,384,256]{3,2,1,0:T(8,128)(2,1)S(1)} %copy-done), custom_call_target="tpu_custom_call" | custom-call | tf_op jit(solution)/shard_map/stacked/pallas_call | solution.py:383
Async XLA Ops:
  46.5 1.7 %copy-start = (bf16[4,3,384,256]{3,2,1,0:T(8,128)(2,1)S(1)}, bf16[4,3,384,256]{3,2,1,0:T(8,128)(2,1)}, u32[]{:S(2)}) copy-start(bf16[4,3,384,256]{3,2,1,0:T(8,128)(2,1)} %get-tuple-element.8.right_ref) | copy-start | bytes 7077892
  48.2 1.4 %copy-start.1 = (bf16[4,512,384]{2,1,0:T(8,128)(2,1)S(1)}, bf16[4,512,384]{2,1,0:T(8,128)(2,1)}, u32[]{:S(2)}) copy-start(bf16[4,512,384]{2,1,0:T(8,128)(2,1)} %get-tuple-element.7.left_ref) | copy-start | bytes 4718596

commit v4 on v3

--- a/solution.py
+++ b/solution.py
@@ -17,7 +17,7 @@
 F32 = jnp.float32
 
 PART_WINDOWS = (8, 4)
-CHUNKS = ((0, 0, 1), (0, 1, 1), (1, 0, 2), (0, 2, 1), (0, 3, 1), (1, 2, 2))
+CHUNKS = ((0, 0, 1), (0, 1, 1), (1, 0, 2), (0, 2, 1), (1, 2, 2), (0, 3, 1))
 
 
 def sin_cos(x):
@@ -60,12 +60,13 @@
 
 
 def exchange(
-    nz, ngrp, map_hbm, bin_hbm, strain_hbm, left_hbm, right_hbm,
-    slab_a, slab_b, left_ref, right_ref, map_ref, bin_ref, strain_ref, load_sem, basis, onehot, wacc, rows_a, rows_b, out_a, out_b, transit_a, transit_b, halo_out, halo_in,
-    halo_send, halo_recv, z_send, z_recv, own_sem, x_send, m_recv, x_recv, r_send, l_send, l_recv, out_sem,
+    nz, ngrp, map_hbm, bin_hbm, strain_hbm, cross_hbm,
+    slab_a, slab_b, via_a, via_b, left_ref, cross_ref, map_ref, bin_ref, strain_ref, load_sem, basis, onehot, wacc, rows_a, rows_b, out_a, out_b, transit_a, transit_b, halo_out, halo_in,
+    halo_send, halo_recv, z_send, z_recv, own_sem, x_send, m_recv, v_send, v_recv, x_recv, r_send, l_send, l_recv, out_sem,
 ):
-    slabs, outs, transits = (slab_a, slab_b), (out_a, out_b), (transit_a, transit_b)
+    slabs, vias, outs, transits = (slab_a, slab_b), (via_a, via_b), (out_a, out_b), (transit_a, transit_b)
     nspan = 2 * nz
+    scale = 1.0 / math.sqrt(nspan * (strain_ref.shape[1] // HOP))
     g, s = lax.axis_index("grp"), lax.axis_index("span")
     z, lo, core = s // 2, s % 2, g % 2
     nb = bin_ref.shape[1]
@@ -99,7 +100,7 @@
     quarter = lax.rem(g, 4)
     relayed = jnp.where(quarter == 1, 1, 0)
     relaying = jnp.where(quarter == 3, 1, 0)
-    hello(at(2 - 4 * relaying, s))
+    side = lax.rem(lo + core, 2)
     hello(at(2 - 4 * relaying, other))
 
     @pl.when(relaying == 1)
@@ -138,7 +139,7 @@
     for j in range(3):
         hop(j)
     halo_out[...] = wacc[0:3].astype(BF)
-    pl.semaphore_wait(barrier, nz - 1 + 6 + relaying)
+    pl.semaphore_wait(barrier, nz - 1 + 5 + relaying)
     halo = pltpu.make_async_remote_copy(
         src_ref=halo_out, dst_ref=halo_in, send_sem=halo_send, recv_sem=halo_recv,
         device_id=at(0, behind), device_id_type=MESH,
@@ -199,10 +200,18 @@
         arrived(transit.at[:, n], z_recv.at[c])
         send(transit.at[1 - lo, n], slab.at[to, lo, n], x_send.at[c, 1], sem, at(dg, other))
         send(transit.at[1 - lo, n], slab.at[0, lo, n], x_send.at[c, 0], m_recv.at[c], at(0, other))
-        send(transit.at[lo, n], slab.at[to, lo, n], x_send.at[c, 2], sem, at(dg, s))
+        send(transit.at[lo, n], vias[part].at[n], x_send.at[c, 2], v_recv.at[c], at(side * dg, other))
         pltpu.make_async_copy(transit.at[lo, n], slab.at[0, lo, n], own_sem.at[c]).start()
 
-    def own_onward(c):
+    def pass_on(c):
+        part, n0, nn = CHUNKS[c]
+        n = pl.ds(n0, nn)
+        arrived(vias[part].at[n], v_recv.at[c])
+        sem = side * relayed + (1 - side) * relaying
+        send(vias[part].at[n], slabs[part].at[2 + 2 * sem, 1 - lo, n], v_send.at[c], x_recv.at[c, sem],
+             at(side * (4 * relayed - 2), other))
+
+    def relay(c):
         part, n0, nn = CHUNKS[c]
         slab = slabs[part]
         n = pl.ds(n0, nn)
@@ -215,6 +224,10 @@
                 send_sem=r_send.at[c], recv_sem=x_recv.at[c, 0], device_id=at(-4, s), device_id_type=MESH,
             ).start()
 
+    def own_onward(c):
+        part, n0, nn = CHUNKS[c]
+        slab = slabs[part]
+        n = pl.ds(n0, nn)
         arrived(slab.at[0, lo, n], own_sem.at[c])
         arrived(slab.at[0, 1 - lo, n], m_recv.at[c])
         to = 3 - 2 * core
@@ -244,12 +257,7 @@
 
     written = []
 
-    def put(src, dst, sem):
-        copy = pltpu.make_async_copy(src, dst, sem)
-        copy.start()
-        written.append(copy)
-
-    def own_bins(bins):
+    def own_bins(*bins):
         for n in bins:
             own = whitened(0, n).astype(F32)
             swapped = pltpu.roll(own.reshape(-1, 8, channels), 4, 1)
@@ -257,12 +265,18 @@
             swapped = jnp.where(imag_row, -swapped, swapped).reshape(own.shape)
             left_ref[n, :channels] = own.T.astype(BF)
             left_ref[n, channels:] = swapped.T.astype(BF)
-            put(left_ref.at[n], left_hbm.at[n], out_sem.at[0, n])
-
-    def next_bins(slot, bins):
+
+    def stack_bins(slot, *bins):
         for n in bins:
-            right_ref[n, slot - 1] = whitened(slot, n)
-            put(right_ref.at[n, slot - 1], right_hbm.at[n, slot - 1], out_sem.at[slot, n])
+            both = jnp.dot(left_ref[n], whitened(slot, n), preferred_element_type=F32)
+            both = (both * scale).astype(BF)
+            cross_ref[slot - 1, n, :, :channels] = both[:channels]
+            cross_ref[slot - 1, n, :, channels:] = both[channels:]
+            copy = pltpu.make_async_copy(
+                cross_ref.at[slot - 1, n], cross_hbm.at[slot - 1, n], out_sem.at[slot - 1, n]
+            )
+            copy.start()
+            written.append(copy)
 
     arrange(0, 0)
     to_slabs(0)
@@ -277,37 +291,53 @@
     across(0)
     to_slabs(4)
     across(1)
+    to_slabs(5)
+    pass_on(0)
     own_onward(0)
-    to_slabs(5)
     across(2)
+    pass_on(1)
     own_onward(1)
+    relay(0)
+    across(3)
+    pass_on(2)
+    own_onward(2)
+    relay(1)
     next_onward(0)
-    across(3)
-    own_onward(2)
+    own_bins(0, 1)
+    across(4)
+    pass_on(3)
+    own_onward(3)
+    relay(2)
     next_onward(1)
-    own_bins((0, 1))
-    across(4)
-    own_onward(3)
+    across(5)
+    pass_on(4)
+    own_onward(4)
+    relay(3)
     next_onward(2)
+    own_bins(2)
+    stack_bins(2, 0, 1)
+    pass_on(5)
+    own_onward(5)
+    relay(4)
+    next_onward(3)
     last(0)
-    next_bins(2, (0, 1))
-    across(5)
-    own_onward(4)
-    next_onward(3)
     last(1)
     last(2)
-    next_bins(1, (0, 1))
-    next_bins(3, (0, 1))
-    own_onward(5)
+    stack_bins(1, 0, 1)
+    stack_bins(3, 0, 1)
+    relay(5)
     next_onward(4)
-    own_bins((2, 3))
+    own_bins(3)
     next_onward(5)
+    stack_bins(2, 2)
     last(3)
     last(4)
-    next_bins(2, (2, 3))
+    stack_bins(1, 2)
+    stack_bins(3, 2)
+    stack_bins(2, 3)
     last(5)
-    next_bins(1, (2, 3))
-    next_bins(3, (2, 3))
+    stack_bins(1, 3)
+    stack_bins(3, 3)
     nc = len(CHUNKS)
     for copy in written:
         copy.wait()
@@ -322,15 +352,6 @@
             part, n0, nn = CHUNKS[c]
             ref = slabs[part].at[4, :, pl.ds(n0, nn)]
             arrived(ref, r_send.at[c])
-
-
-def stacked(scale, left_ref, right_ref, o_ref):
-    ch = right_ref.shape[-1]
-    for r in range(ROUNDS):
-        both = jnp.dot(left_ref[0], right_ref[0, r], preferred_element_type=F32)
-        both = (both * scale).astype(BF)
-        o_ref[r, 0, :, :ch] = both[:ch]
-        o_ref[r, 0, :, ch:] = both[ch:]
 
 
 def local(strain, channel_map, bin_index):
@@ -344,19 +365,18 @@
     nc = len(CHUNKS)
     dma = pltpu.SemaphoreType.DMA
     depth = nspan * sum(rows)
-    left, right = pl.pallas_call(
+    return pl.pallas_call(
         functools.partial(exchange, nz, ngrp),
-        out_shape=[
-            jax.ShapeDtypeStruct((per, 2 * channels, depth), BF),
-            jax.ShapeDtypeStruct((per, ROUNDS, depth, channels), BF),
-        ],
+        out_shape=jax.ShapeDtypeStruct((ROUNDS, per, channels, 2 * channels), BF),
         in_specs=[pl.BlockSpec(memory_space=pltpu.HBM)] * 3,
-        out_specs=[pl.BlockSpec(memory_space=pl.ANY)] * 2,
+        out_specs=pl.BlockSpec(memory_space=pl.ANY),
         scratch_shapes=[
             pltpu.VMEM((ROUNDS + 2, 2, per, nz, rows[0], channels), BF),
             pltpu.VMEM((ROUNDS + 2, 2, per, nz, rows[1], channels), BF),
+            pltpu.VMEM((per, nz, rows[0], channels), BF),
+            pltpu.VMEM((per, nz, rows[1], channels), BF),
             pltpu.VMEM((per, 2 * channels, depth), BF),
-            pltpu.VMEM((per, ROUNDS, depth, channels), BF),
+            pltpu.VMEM((ROUNDS, per, channels, 2 * channels), BF),
             pltpu.VMEM((1, channels), jnp.int32),
             pltpu.VMEM((1, nb), jnp.int32),
             pltpu.VMEM((channels, strain.shape[1]), BF),
@@ -372,26 +392,13 @@
             pltpu.VMEM((2, per, nz, rows[1], channels), BF),
             pltpu.VMEM((3, 2 * nb, channels), BF),
             pltpu.VMEM((3, 2 * nb, channels), BF),
-            dma, dma, dma((2,)), dma((nc,)), dma((nc,)), dma((nc, 3)), dma((nc,)), dma((nc, 2)), dma((nc,)), dma((nc, 2)), dma((nc, 2)), dma((ROUNDS + 1, per)),
+            dma, dma, dma((2,)), dma((nc,)), dma((nc,)), dma((nc, 3)), dma((nc,)), dma((nc,)), dma((nc,)), dma((nc, 2)), dma((nc,)), dma((nc, 2)), dma((nc, 2)), dma((ROUNDS, per)),
         ],
         compiler_params=pltpu.CompilerParams(
             collective_id=0, has_side_effects=True, vmem_limit_bytes=58_000_000
         ),
         name="exchange",
     )(channel_map, bin_index.reshape(1, nb), strain)
-
-    return pl.pallas_call(
-        functools.partial(stacked, 1.0 / math.sqrt(win * nspan)),
-        grid=(per,),
-        in_specs=[
-            pl.BlockSpec((1, 2 * channels, depth), lambda i: (i, 0, 0)),
-            pl.BlockSpec((1, ROUNDS, depth, channels), lambda i: (i, 0, 0, 0)),
-        ],
-        out_specs=pl.BlockSpec((ROUNDS, 1, channels, 2 * channels), lambda i: (0, i, 0, 0)),
-        out_shape=jax.ShapeDtypeStruct((ROUNDS, per, channels, 2 * channels), BF),
-        compiler_params=pltpu.CompilerParams(vmem_limit_bytes=32 * 2**20),
-        name="stacked",
-    )(left, right)
 
 
 def solution(mesh):

time: 53.3 us -> 56 us (1.051)
  the two profiles are of different devices: /device:TPU:31 before, /device:TPU:13 now
where the time goes in v4:
time: 56 us; the launch traced here: 55.8 us
  Pallas kernels  52 us (93%)
  local copies, waits for them, and re-layouts  3.76 us (7%)
    pallas_call x1, Pallas kernels, local(): pl.pallas_call(functools.partial(exchange, nz, ngrp), out_shape=jax.Shape...  52 us
    unnamed x1, local copies, waits for them, and re-layouts  3.76 us

profile of v4, /device:TPU:13, one launch (start us, length us, event | category | flops | bytes accessed | tf_op | source)
XLA Modules:
  0.0 55.8 jit_solution(2707916394622469872)
XLA Ops:
  0.0 52.0 %exchange.1 = bf16[3,4,256,512]{3,2,1,0:T(8,128)(2,1)} custom-call(s32[1,256]{1,0:T(1,128)} %map_hbm.1, s32[1,64]{1,0:T(1,128)} %bitcast.1, bf16[256,3072]{1,0:T(8,128)(2,1)} %strain_hbm.1), custom_call_target="tpu_custom_call" | custom-call | tf_op jit(solution)/shard_map/exchange/pallas_call | solution.py:368
  52.1 3.8 %copy.5 = bf16[3,4,256,512]{3,2,1,0:T(8,128)(2,1)} copy(bf16[3,4,256,512]{3,2,1,0:T(8,128)(2,1)} %exchange.1) | data formatting | bytes 6291456

commit v5 on v4

--- a/solution.py
+++ b/solution.py
@@ -60,13 +60,12 @@
 
 
 def exchange(
-    nz, ngrp, map_hbm, bin_hbm, strain_hbm, cross_hbm,
-    slab_a, slab_b, via_a, via_b, left_ref, cross_ref, map_ref, bin_ref, strain_ref, load_sem, basis, onehot, wacc, rows_a, rows_b, out_a, out_b, transit_a, transit_b, halo_out, halo_in,
-    halo_send, halo_recv, z_send, z_recv, own_sem, x_send, m_recv, v_send, v_recv, x_recv, r_send, l_send, l_recv, out_sem,
+    nz, ngrp, map_hbm, bin_hbm, strain_hbm, left_ref, right_ref,
+    slab_a, slab_b, map_ref, bin_ref, strain_ref, load_sem, basis, onehot, wacc, rows_a, rows_b, out_a, out_b, transit_a, transit_b, halo_out, halo_in,
+    halo_send, halo_recv, z_send, z_recv, own_sem, x_send, m_recv, x_recv, r_send, l_send, l_recv,
 ):
-    slabs, vias, outs, transits = (slab_a, slab_b), (via_a, via_b), (out_a, out_b), (transit_a, transit_b)
+    slabs, outs, transits = (slab_a, slab_b), (out_a, out_b), (transit_a, transit_b)
     nspan = 2 * nz
-    scale = 1.0 / math.sqrt(nspan * (strain_ref.shape[1] // HOP))
     g, s = lax.axis_index("grp"), lax.axis_index("span")
     z, lo, core = s // 2, s % 2, g % 2
     nb = bin_ref.shape[1]
@@ -100,7 +99,7 @@
     quarter = lax.rem(g, 4)
     relayed = jnp.where(quarter == 1, 1, 0)
     relaying = jnp.where(quarter == 3, 1, 0)
-    side = lax.rem(lo + core, 2)
+    hello(at(2 - 4 * relaying, s))
     hello(at(2 - 4 * relaying, other))
 
     @pl.when(relaying == 1)
@@ -139,7 +138,7 @@
     for j in range(3):
         hop(j)
     halo_out[...] = wacc[0:3].astype(BF)
-    pl.semaphore_wait(barrier, nz - 1 + 5 + relaying)
+    pl.semaphore_wait(barrier, nz - 1 + 6 + relaying)
     halo = pltpu.make_async_remote_copy(
         src_ref=halo_out, dst_ref=halo_in, send_sem=halo_send, recv_sem=halo_recv,
         device_id=at(0, behind), device_id_type=MESH,
@@ -168,8 +167,7 @@
         pltpu.make_async_copy(out.at[z, :, n], transit.at[:, n, z], z_recv.at[c]).start()
 
         def step(i, _):
-            off = (i + 1) // 2
-            there = lax.rem(z + nz // 2 + off * (1 - 2 * (i % 2)), nz)
+            there = i + jnp.where(i >= z, 1, 0)
             pltpu.make_async_remote_copy(
                 src_ref=out.at[there, :, n], dst_ref=transit.at[:, n, z],
                 send_sem=z_send.at[part], recv_sem=z_recv.at[c],
@@ -200,16 +198,8 @@
         arrived(transit.at[:, n], z_recv.at[c])
         send(transit.at[1 - lo, n], slab.at[to, lo, n], x_send.at[c, 1], sem, at(dg, other))
         send(transit.at[1 - lo, n], slab.at[0, lo, n], x_send.at[c, 0], m_recv.at[c], at(0, other))
-        send(transit.at[lo, n], vias[part].at[n], x_send.at[c, 2], v_recv.at[c], at(side * dg, other))
+        send(transit.at[lo, n], slab.at[to, lo, n], x_send.at[c, 2], sem, at(dg, s))
         pltpu.make_async_copy(transit.at[lo, n], slab.at[0, lo, n], own_sem.at[c]).start()
-
-    def pass_on(c):
-        part, n0, nn = CHUNKS[c]
-        n = pl.ds(n0, nn)
-        arrived(vias[part].at[n], v_recv.at[c])
-        sem = side * relayed + (1 - side) * relaying
-        send(vias[part].at[n], slabs[part].at[2 + 2 * sem, 1 - lo, n], v_send.at[c], x_recv.at[c, sem],
-             at(side * (4 * relayed - 2), other))
 
     def relay(c):
         part, n0, nn = CHUNKS[c]
@@ -254,8 +244,6 @@
         v = jnp.concatenate([a.reshape(-1, channels), b.reshape(-1, channels)], axis=0)
         power = jnp.sum(v * v, axis=0, keepdims=True) * (1.0 / v.shape[0])
         return (v * lax.rsqrt(power + epsilon)).astype(BF)
-
-    written = []
 
     def own_bins(*bins):
         for n in bins:
@@ -266,17 +254,9 @@
             left_ref[n, :channels] = own.T.astype(BF)
             left_ref[n, channels:] = swapped.T.astype(BF)
 
-    def stack_bins(slot, *bins):
+    def next_bins(slot, *bins):
         for n in bins:
-            both = jnp.dot(left_ref[n], whitened(slot, n), preferred_element_type=F32)
-            both = (both * scale).astype(BF)
-            cross_ref[slot - 1, n, :, :channels] = both[:channels]
-            cross_ref[slot - 1, n, :, channels:] = both[channels:]
-            copy = pltpu.make_async_copy(
-                cross_ref.at[slot - 1, n], cross_hbm.at[slot - 1, n], out_sem.at[slot - 1, n]
-            )
-            copy.start()
-            written.append(copy)
+            right_ref[n, slot - 1] = whitened(slot, n)
 
     arrange(0, 0)
     to_slabs(0)
@@ -292,55 +272,47 @@
     to_slabs(4)
     across(1)
     to_slabs(5)
-    pass_on(0)
     own_onward(0)
     across(2)
-    pass_on(1)
     own_onward(1)
     relay(0)
     across(3)
-    pass_on(2)
     own_onward(2)
     relay(1)
     next_onward(0)
     own_bins(0, 1)
     across(4)
-    pass_on(3)
     own_onward(3)
     relay(2)
     next_onward(1)
     across(5)
-    pass_on(4)
     own_onward(4)
     relay(3)
     next_onward(2)
     own_bins(2)
-    stack_bins(2, 0, 1)
-    pass_on(5)
+    next_bins(2, 0, 1)
     own_onward(5)
     relay(4)
     next_onward(3)
     last(0)
     last(1)
     last(2)
-    stack_bins(1, 0, 1)
-    stack_bins(3, 0, 1)
+    next_bins(1, 0, 1)
+    next_bins(3, 0, 1)
     relay(5)
     next_onward(4)
     own_bins(3)
     next_onward(5)
-    stack_bins(2, 2)
+    next_bins(2, 2)
     last(3)
     last(4)
-    stack_bins(1, 2)
-    stack_bins(3, 2)
-    stack_bins(2, 3)
+    next_bins(1, 2)
+    next_bins(3, 2)
+    next_bins(2, 3)
     last(5)
-    stack_bins(1, 3)
-    stack_bins(3, 3)
+    next_bins(1, 3)
+    next_bins(3, 3)
     nc = len(CHUNKS)
-    for copy in written:
-        copy.wait()
     for part in range(2):
         arrived(outs[part].at[pl.ds(0, nz - 1)], z_send.at[part])
     for copy in sent:
@@ -352,6 +324,22 @@
             part, n0, nn = CHUNKS[c]
             ref = slabs[part].at[4, :, pl.ds(n0, nn)]
             arrived(ref, r_send.at[c])
+
+
+def stacked(scale, left_ref, right_ref, cross_hbm, cross_ref, sem):
+    bins, ch = right_ref.shape[0], right_ref.shape[-1]
+    copies = []
+    for n in range(bins):
+        for r in range(ROUNDS):
+            both = jnp.dot(left_ref[n], right_ref[n, r], preferred_element_type=F32)
+            both = (both * scale).astype(BF)
+            cross_ref[r, n, :, :ch] = both[:ch]
+            cross_ref[r, n, :, ch:] = both[ch:]
+            copy = pltpu.make_async_copy(cross_ref.at[r, n], cross_hbm.at[r, n], sem.at[r, n])
+            copy.start()
+            copies.append(copy)
+    for copy in copies:
+        copy.wait()
 
 
 def local(strain, channel_map, bin_index):
@@ -365,18 +353,17 @@
     nc = len(CHUNKS)
     dma = pltpu.SemaphoreType.DMA
     depth = nspan * sum(rows)
-    return pl.pallas_call(
+    left, right = pl.pallas_call(
         functools.partial(exchange, nz, ngrp),
-        out_shape=jax.ShapeDtypeStruct((ROUNDS, per, channels, 2 * channels), BF),
+        out_shape=[
+            pltpu.VMEM((per, 2 * channels, depth), BF),
+            pltpu.VMEM((per, ROUNDS, depth, channels), BF),
+        ],
         in_specs=[pl.BlockSpec(memory_space=pltpu.HBM)] * 3,
-        out_specs=pl.BlockSpec(memory_space=pl.ANY),
+        out_specs=[pl.BlockSpec(memory_space=pltpu.VMEM)] * 2,
         scratch_shapes=[
             pltpu.VMEM((ROUNDS + 2, 2, per, nz, rows[0], channels), BF),
             pltpu.VMEM((ROUNDS + 2, 2, per, nz, rows[1], channels), BF),
-            pltpu.VMEM((per, nz, rows[0], channels), BF),
-            pltpu.VMEM((per, nz, rows[1], channels), BF),
-            pltpu.VMEM((per, 2 * channels, depth), BF),
-            pltpu.VMEM((ROUNDS, per, channels, 2 * channels), BF),
             pltpu.VMEM((1, channels), jnp.int32),
             pltpu.VMEM((1, nb), jnp.int32),
             pltpu.VMEM((channels, strain.shape[1]), BF),
@@ -392,13 +379,24 @@
             pltpu.VMEM((2, per, nz, rows[1], channels), BF),
             pltpu.VMEM((3, 2 * nb, channels), BF),
             pltpu.VMEM((3, 2 * nb, channels), BF),
-            dma, dma, dma((2,)), dma((nc,)), dma((nc,)), dma((nc, 3)), dma((nc,)), dma((nc,)), dma((nc,)), dma((nc, 2)), dma((nc,)), dma((nc, 2)), dma((nc, 2)), dma((ROUNDS, per)),
+            dma, dma, dma((2,)), dma((nc,)), dma((nc,)), dma((nc, 3)), dma((nc,)), dma((nc, 2)), dma((nc,)), dma((nc, 2)), dma((nc, 2)),
         ],
         compiler_params=pltpu.CompilerParams(
-            collective_id=0, has_side_effects=True, vmem_limit_bytes=58_000_000
+            collective_id=0, has_side_effects=True, vmem_limit_bytes=53_000_000
         ),
         name="exchange",
     )(channel_map, bin_index.reshape(1, nb), strain)
+
+    result = (ROUNDS, per, channels, 2 * channels)
+    return pl.pallas_call(
+        functools.partial(stacked, 1.0 / math.sqrt(win * nspan)),
+        in_specs=[pl.BlockSpec(memory_space=pltpu.VMEM)] * 2,
+        out_specs=pl.BlockSpec(memory_space=pl.ANY),
+        out_shape=jax.ShapeDtypeStruct(result, BF),
+        scratch_shapes=[pltpu.VMEM(result, BF), dma((ROUNDS, per))],
+        compiler_params=pltpu.CompilerParams(vmem_limit_bytes=32 * 2**20),
+        name="stacked",
+    )(left, right)
 
 
 def solution(mesh):

time: 56 us -> 48 us (0.86)
  the two profiles are of different devices: /device:TPU:13 before, /device:TPU:31 now
where the time goes in v5:
time: 48 us; the launch traced here: 47.8 us
  Pallas kernels  47.8 us (100%)
    pallas_call x1, Pallas kernels, local(): pl.pallas_call(functools.partial(exchange, nz, ngrp), out_shape=[pltpu.VM...  45.1 us
    pallas_call x1, Pallas kernels, local(): pl.pallas_call(functools.partial(stacked, 1.0 / math.sqrt(win * nspan)),...  2.72 us

profile of v5, /device:TPU:31, one launch (start us, length us, event | category | flops | bytes accessed | tf_op | source)
XLA Modules:
  0.0 47.8 jit_solution(12499027692108849773)
XLA Ops:
  0.0 45.1 %exchange.1 = (bf16[4,512,384]{2,1,0:T(8,128)(2,1)S(1)}, bf16[4,3,384,256]{3,2,1,0:T(8,128)(2,1)S(1)}) custom-call(s32[1,256]{1,0:T(1,128)} %map_hbm.1, s32[1,64]{1,0:T(1,128)} %bitcast.1, bf16[256,3072]{1,0:T(8,128)(2,1)} %strain_hbm.1), custom_call_target="tpu_custom_call" | custom-call | tf_op jit(solution)/shard_map/exchange/pallas_call | solution.py:356
  45.1 2.7 %stacked.1 = bf16[3,4,256,512]{3,2,1,0:T(8,128)(2,1)} custom-call(bf16[4,512,384]{2,1,0:T(8,128)(2,1)S(1)} %get-tuple-element.7.left_ref, bf16[4,3,384,256]{3,2,1,0:T(8,128)(2,1)S(1)} %get-tuple-element.8.right_ref), custom_call_target="tpu_custom_call" | custom-call | tf_op jit(solution)/shard_map/stacked/pallas_call | solution.py:391

commit v6 on v5

--- a/solution.py
+++ b/solution.py
@@ -34,10 +34,11 @@
     return jnp.where(odd, s, c) * cos_sign, jnp.where(odd, c, s) * sin_sign
 
 
-def fill_basis(bin_ref, basis):
+def fill_basis(bin_ref, basis, nspan):
     nb = bin_ref.shape[1]
     row = lax.broadcasted_iota(jnp.int32, (nb, nb), 0)
     col = lax.broadcasted_iota(jnp.int32, (nb, nb), 1)
+    row = lax.rem(row, nspan) * (nb // nspan) + row // nspan
     bins = jnp.where(row == col, jnp.broadcast_to(bin_ref[...].astype(F32), (nb, nb)), 0.0)
     bins = jnp.sum(bins, axis=1, keepdims=True).astype(jnp.int32)
     t = lax.broadcasted_iota(jnp.int32, (nb, HOP), 1)
@@ -116,10 +117,7 @@
     lax.fori_loop(1, nz, hello_z, 0)
 
     loads[0].wait()
-    fill_basis(bin_ref, basis)
-    loads[1].wait()
-    c_in = lax.broadcasted_iota(jnp.int32, (channels, channels), 0)
-    onehot[...] = jnp.where(c_in == jnp.broadcast_to(map_ref[...], (channels, channels)), 1.0, 0.0).astype(BF)
+    fill_basis(bin_ref, basis, nspan)
 
     def hop(j):
         loads[2 + j].wait()
@@ -144,21 +142,28 @@
         device_id=at(0, behind), device_id_type=MESH,
     )
     halo.start()
+    loads[1].wait()
+    c_in = lax.broadcasted_iota(jnp.int32, (channels, channels), 0)
+    onehot[...] = jnp.where(c_in == jnp.broadcast_to(map_ref[...], (channels, channels)), 1.0, 0.0).astype(BF)
     for j in range(3, win):
         hop(j)
 
-    def arrange(part, first):
+    def arrange(part, first, n):
         rows, out = (rows_a, rows_b)[part], outs[part]
         per = 2 * PART_WINDOWS[part]
+        base = n * nspan * per
         for w in range(PART_WINDOWS[part]):
             for p in range(2):
-                at_row = (w // 4) * 8 + p * 4 + w % 4
-                piece = wacc[3 + first + w, p * nb : (p + 1) * nb, :]
+                at_row = base + (w // 4) * 8 + p * 4 + w % 4
+                k = p * nb + n * nspan
+                piece = wacc[3 + first + w, k : k + nspan, :]
                 for h in range(channels // 128):
-                    rows[h, pl.ds(at_row, nb, stride=per), :] = piece[:, h * 128 : (h + 1) * 128]
-        by_map = jnp.concatenate([rows[h].astype(BF) for h in range(channels // 128)], axis=1)
+                    rows[h, pl.ds(at_row, nspan, stride=per), :] = piece[:, h * 128 : (h + 1) * 128]
+        by_map = jnp.concatenate(
+            [rows[h, base : base + nspan * per].astype(BF) for h in range(channels // 128)], axis=1
+        )
         ordered = jnp.dot(by_map, onehot[...], preferred_element_type=F32)
-        out[...] = ordered.reshape(out.shape).astype(BF)
+        out[:, :, n] = ordered.reshape(nz, 2, per, channels).astype(BF)
 
     def to_slabs(c):
         part, n0, nn = CHUNKS[c]
@@ -258,16 +263,22 @@
         for n in bins:
             right_ref[n, slot - 1] = whitened(slot, n)
 
-    arrange(0, 0)
+    arrange(0, 0, 0)
     to_slabs(0)
+    arrange(0, 0, 1)
     to_slabs(1)
+    arrange(0, 0, 2)
+    arrange(0, 0, 3)
     halo.wait()
     keep = jnp.where(s == nspan - 1, 0.0, 1.0)
     for i in range(3):
         wacc[win + i] = wacc[win + i] + halo_in[i].astype(F32) * keep
-    arrange(1, PART_WINDOWS[0])
+    arrange(1, PART_WINDOWS[0], 0)
+    arrange(1, PART_WINDOWS[0], 1)
     to_slabs(2)
     to_slabs(3)
+    arrange(1, PART_WINDOWS[0], 2)
+    arrange(1, PART_WINDOWS[0], 3)
     across(0)
     to_slabs(4)
     across(1)

time: 48 us -> 48.1 us (level)
  no operation moved by 1% of the time
where the time goes in v6:
time: 48.1 us; the launch traced here: 47.9 us
  Pallas kernels  47.9 us (100%)
    pallas_call x1, Pallas kernels, local(): pl.pallas_call(functools.partial(exchange, nz, ngrp), out_shape=[pltpu.VM...  45.2 us
    pallas_call x1, Pallas kernels, local(): pl.pallas_call(functools.partial(stacked, 1.0 / math.sqrt(win * nspan)),...  2.72 us

profile of v6, /device:TPU:31, one launch (start us, length us, event | category | flops | bytes accessed | tf_op | source)
XLA Modules:
  0.0 47.9 jit_solution(2896389439142933316)
XLA Ops:
  0.0 45.2 %exchange.1 = (bf16[4,512,384]{2,1,0:T(8,128)(2,1)S(1)}, bf16[4,3,384,256]{3,2,1,0:T(8,128)(2,1)S(1)}) custom-call(s32[1,256]{1,0:T(1,128)} %map_hbm.1, s32[1,64]{1,0:T(1,128)} %bitcast.1, bf16[256,3072]{1,0:T(8,128)(2,1)} %strain_hbm.1), custom_call_target="tpu_custom_call" | custom-call | tf_op jit(solution)/shard_map/exchange/pallas_call | solution.py:367
  45.2 2.7 %stacked.1 = bf16[3,4,256,512]{3,2,1,0:T(8,128)(2,1)} custom-call(bf16[4,512,384]{2,1,0:T(8,128)(2,1)S(1)} %get-tuple-element.7.left_ref, bf16[4,3,384,256]{3,2,1,0:T(8,128)(2,1)S(1)} %get-tuple-element.8.right_ref), custom_call_target="tpu_custom_call" | custom-call | tf_op jit(solution)/shard_map/stacked/pallas_call | solution.py:402

commit v7 on v5

--- a/solution.py
+++ b/solution.py
@@ -17,6 +17,7 @@
 F32 = jnp.float32
 
 PART_WINDOWS = (8, 4)
+DIRECT = (0,)
 CHUNKS = ((0, 0, 1), (0, 1, 1), (1, 0, 2), (0, 2, 1), (1, 2, 2), (0, 3, 1))
 
 
@@ -105,6 +106,8 @@
     @pl.when(relaying == 1)
     def _():
         hello(at(4, s))
+        hello(at(2, s))
+        hello(at(2, other))
 
     hello(at(1 + 2 * core, s))
     hello(at(1 - 2 * core, s))
@@ -138,7 +141,7 @@
     for j in range(3):
         hop(j)
     halo_out[...] = wacc[0:3].astype(BF)
-    pl.semaphore_wait(barrier, nz - 1 + 6 + relaying)
+    pl.semaphore_wait(barrier, nz - 1 + 6 + relaying + 2 * relayed)
     halo = pltpu.make_async_remote_copy(
         src_ref=halo_out, dst_ref=halo_in, send_sem=halo_send, recv_sem=halo_recv,
         device_id=at(0, behind), device_id_type=MESH,
@@ -194,7 +197,8 @@
         part, n0, nn = CHUNKS[c]
         slab, transit = slabs[part], transits[part]
         n = pl.ds(n0, nn)
-        to, dg, sem = 2 + 2 * relayed, 4 * relayed - 2, x_recv.at[c, relayed]
+        by = 0 if c in DIRECT else relayed
+        to, dg, sem = 2 + 2 * by, 4 * by - 2, x_recv.at[c, by]
         arrived(transit.at[:, n], z_recv.at[c])
         send(transit.at[1 - lo, n], slab.at[to, lo, n], x_send.at[c, 1], sem, at(dg, other))
         send(transit.at[1 - lo, n], slab.at[0, lo, n], x_send.at[c, 0], m_recv.at[c], at(0, other))
@@ -274,35 +278,34 @@
     to_slabs(5)
     own_onward(0)
     across(2)
+    relay(1)
     own_onward(1)
-    relay(0)
+    next_onward(0)
     across(3)
+    relay(2)
     own_onward(2)
-    relay(1)
-    next_onward(0)
+    next_onward(1)
     own_bins(0, 1)
     across(4)
+    relay(3)
     own_onward(3)
-    relay(2)
-    next_onward(1)
+    next_onward(2)
     across(5)
+    relay(4)
     own_onward(4)
-    relay(3)
-    next_onward(2)
-    own_bins(2)
+    next_onward(3)
     next_bins(2, 0, 1)
-    own_onward(5)
-    relay(4)
-    next_onward(3)
     last(0)
     last(1)
     last(2)
     next_bins(1, 0, 1)
+    relay(5)
+    own_onward(5)
+    next_onward(4)
     next_bins(3, 0, 1)
-    relay(5)
-    next_onward(4)
+    own_bins(2)
+    next_onward(5)
     own_bins(3)
-    next_onward(5)
     next_bins(2, 2)
     last(3)
     last(4)
@@ -321,6 +324,8 @@
     @pl.when(relaying == 1)
     def _():
         for c in range(nc):
+            if c in DIRECT:
+                continue
             part, n0, nn = CHUNKS[c]
             ref = slabs[part].at[4, :, pl.ds(n0, nn)]
             arrived(ref, r_send.at[c])

time: 48 us -> 47.8 us (level)
  no operation moved by 1% of the time
where the time goes in v7:
time: 47.8 us; the launch traced here: 47.6 us
  Pallas kernels  47.6 us (100%)
    pallas_call x1, Pallas kernels, local(): pl.pallas_call(functools.partial(exchange, nz, ngrp), out_shape=[pltpu.VM...  44.9 us
    pallas_call x1, Pallas kernels, local(): pl.pallas_call(functools.partial(stacked, 1.0 / math.sqrt(win * nspan)),...  2.71 us

profile of v7, /device:TPU:31, one launch (start us, length us, event | category | flops | bytes accessed | tf_op | source)
XLA Modules:
  0.0 47.6 jit_solution(10428245440312646514)
XLA Ops:
  0.0 44.9 %exchange.1 = (bf16[4,512,384]{2,1,0:T(8,128)(2,1)S(1)}, bf16[4,3,384,256]{3,2,1,0:T(8,128)(2,1)S(1)}) custom-call(s32[1,256]{1,0:T(1,128)} %map_hbm.1, s32[1,64]{1,0:T(1,128)} %bitcast.1, bf16[256,3072]{1,0:T(8,128)(2,1)} %strain_hbm.1), custom_call_target="tpu_custom_call" | custom-call | tf_op jit(solution)/shard_map/exchange/pallas_call | solution.py:361
  44.9 2.7 %stacked.1 = bf16[3,4,256,512]{3,2,1,0:T(8,128)(2,1)} custom-call(bf16[4,512,384]{2,1,0:T(8,128)(2,1)S(1)} %get-tuple-element.7.left_ref, bf16[4,3,384,256]{3,2,1,0:T(8,128)(2,1)S(1)} %get-tuple-element.8.right_ref), custom_call_target="tpu_custom_call" | custom-call | tf_op jit(solution)/shard_map/stacked/pallas_call | solution.py:396
